TPU v7x, 512 devices: a whole 4x8x8 slice. The times are simulated.
512 devices in a mesh: wide: 64 (over x, y, core), grp: 8 (over z).
Axes of the slice: x: 4, y: 8, z: 8, core: 2. Of those that a mesh axis runs over, the one named last changes fastest.
Arguments:
- dense_features: bfloat16 [65536, 128], P(('wide', 'grp')), may hold values from -6 to 6
- bag_slots: int32 [16, 65536, 8], P('grp', 'wide'), may hold values from 0 to 3071, as said below
- cold_offset: int32 [8, 64, 64, 16], P('grp', 'wide'), may hold values from -1 to 1023, as said below
- hot_rows: float32 [8, 2048, 128], P('grp'), may hold values from -2 to 2
- hot_accum: float32 [8, 2048], P('grp'), may hold values from 0.0001 to 0.01
- cold_rows: float32 [8, 65536, 128], P('grp', 'wide'), may hold values from -2 to 2
- cold_accum: float32 [8, 65536], P('grp', 'wide'), may hold values from 0.0001 to 0.01
- cross_down: bfloat16 [2176, 512], P('wide'), may hold values from -0.125 to 0.125
- cross_up: bfloat16 [512, 2176], P('wide'), may hold values from -0.25 to 0.25
- cross_bias: float32 [2176], replicated, may hold values from -3 to 3
- out_weight: bfloat16 [2176], replicated, may hold values from -0.125 to 0.125
- labels: int32 [65536], P(('wide', 'grp')), may hold values from 0 to 1
Outputs:
- logits: float32 [65536], P(('wide', 'grp'))
- new_hot_rows: float32 [8, 2048, 128], P('grp')
- new_hot_accum: float32 [8, 2048], P('grp')
- new_cold_rows: float32 [8, 65536, 128], P('grp', 'wide')
- new_cold_accum: float32 [8, 65536], P('grp', 'wide')
Inputs may be any that keep to these rules, and one draw needn't show every extreme that they name: `bag_slots`: an entry below 2048 names a hot row of the group of its table; an entry 2048 + p * 16 + s names the row fetched by slot s of the request list of its block to owner p, and that slot is live. `cold_offset`: each list to one owner holds its live offsets first and -1 in the rest; some owner receives 16 live slots from every requester of its group.
All inputs are finite; a program needn't handle non-finite values.
Results may differ from a plain program's by a relative error of at most 0.0052.
Values may be sent and summed in bfloat16 or wider, within the bound.
A program may use at most 64 MiB of HBM per device.

v0:
```python
import math

import jax
import jax.numpy as jnp
from jax import lax
from jax.sharding import PartitionSpec as P

LEARN = 0.1
EPSILON = 1e-08


def adagrad(table_rows, accumulator, gradient):
    new_accumulator = accumulator + jnp.mean(gradient * gradient, axis=-1)
    new_rows = table_rows - LEARN * gradient / (jnp.sqrt(new_accumulator)[..., None] + EPSILON)
    return (new_rows, new_accumulator)


def slot_counts(slot_ids, slot_total):
    columns = jnp.arange(slot_total, dtype=jnp.int32)
    counts = jnp.zeros(slot_ids.shape[:2] + (slot_total,), jnp.bfloat16)
    for lookup in range(slot_ids.shape[2]):
        counts = counts + (slot_ids[:, :, lookup, None] == columns).astype(jnp.bfloat16)
    return counts


def split_blocks(array, block_rows):
    tables_here, total_rows = (array.shape[0], array.shape[1])
    pieces = array.reshape((tables_here, total_rows // block_rows, block_rows) + array.shape[2:])
    return jnp.moveaxis(pieces, 1, 0)


def contract_last(left, right):
    return lax.dot_general(
        left, right, (((1,), (1,)), ((), ())), preferred_element_type=jnp.float32
    )


def on_device(
    dense_features,
    bag_slots,
    cold_offset,
    hot_rows,
    hot_accum,
    cold_rows,
    cold_accum,
    cross_down,
    cross_up,
    cross_bias,
    out_weight,
    labels,
):
    tables_here, total_rows, pool_size = bag_slots.shape
    sample_count, row_width = dense_features.shape
    hot_count = hot_rows.shape[1]
    owned_rows = cold_rows.shape[1]
    block_rows = math.gcd(total_rows, 512)
    store_bf = cold_rows[0].astype(jnp.bfloat16)
    asked_rows = lax.all_to_all(cold_offset[0, 0], "wide", split_axis=0, concat_axis=0, tiled=True)
    picked = store_bf[jnp.maximum(asked_rows, 0)]
    picked = jnp.where(asked_rows[..., None] >= 0, picked, jnp.zeros((), jnp.bfloat16))
    returned = lax.all_to_all(picked, "wide", split_axis=0, concat_axis=0, tiled=True)
    fetched, asked_rows = (returned, asked_rows)
    buffer = jnp.concatenate(
        [hot_rows[0].astype(jnp.bfloat16), fetched.reshape(-1, row_width)], axis=0
    )
    slot_total = buffer.shape[0]
    slot_pieces = split_blocks(bag_slots, block_rows)

    def pool_block(slot_block):
        counts = slot_counts(slot_block, slot_total)
        return jnp.einsum("tbs,se->tbe", counts, buffer, preferred_element_type=jnp.float32).astype(
            jnp.bfloat16
        )

    pooled_pieces = lax.map(pool_block, slot_pieces)
    pooled_local = jnp.moveaxis(pooled_pieces, 0, 1).reshape(tables_here, total_rows, row_width)
    pooled = lax.all_to_all(pooled_local, "grp", split_axis=1, concat_axis=0, tiled=True)
    all_tables = pooled.shape[0]
    stacked = jnp.concatenate(
        [
            dense_features,
            jnp.transpose(pooled, (1, 0, 2)).reshape(sample_count, all_tables * row_width),
        ],
        axis=1,
    )
    stacked_wide = stacked.astype(jnp.float32)
    down_full, up_full = (
        lax.all_gather(cross_down, "wide", axis=0, tiled=True),
        lax.all_gather(cross_up, "wide", axis=0, tiled=True),
    )
    low_rank = jnp.dot(stacked, down_full, preferred_element_type=jnp.float32).astype(jnp.bfloat16)
    cross_gain = jnp.dot(low_rank, up_full, preferred_element_type=jnp.float32) + cross_bias
    crossed = stacked_wide * cross_gain + stacked_wide
    head_weight = out_weight.astype(jnp.float32)
    logits = jnp.sum(crossed * head_weight, axis=1)
    residual_grad = jax.nn.sigmoid(logits) - labels.astype(jnp.float32)
    d_crossed = residual_grad[:, None] * head_weight
    d_gain = (d_crossed * stacked_wide).astype(jnp.bfloat16)
    d_low = contract_last(d_gain, up_full).astype(jnp.bfloat16)
    back_term = contract_last(d_low, down_full)
    d_stacked = d_crossed * (cross_gain + 1.0) + back_term
    d_pooled = jnp.transpose(
        d_stacked[:, row_width:].reshape(sample_count, all_tables, row_width), (1, 0, 2)
    ).astype(jnp.bfloat16)
    d_local = lax.all_to_all(d_pooled, "grp", split_axis=0, concat_axis=1, tiled=True)
    grad_pieces = split_blocks(d_local, block_rows)

    def grad_block(total, pair):
        slot_block, grad_rows = pair
        counts = slot_counts(slot_block, slot_total)
        return (
            total
            + jnp.einsum("tbs,tbe->se", counts, grad_rows, preferred_element_type=jnp.float32),
            None,
        )

    slot_grad, unused = lax.scan(
        grad_block, jnp.zeros((slot_total, row_width), jnp.float32), (slot_pieces, grad_pieces)
    )
    hot_grad = slot_grad[:hot_count]
    cold_part = slot_grad[hot_count:].reshape(fetched.shape[0], fetched.shape[1], row_width)
    arrived = lax.all_to_all(cold_part, "wide", split_axis=0, concat_axis=0, tiled=True)
    target = jnp.where(asked_rows >= 0, asked_rows, owned_rows)
    cold_grad = (
        jnp.zeros((owned_rows, row_width), jnp.float32)
        .at[target.reshape(-1)]
        .add(arrived.reshape(-1, row_width), mode="drop")
    )
    new_cold_rows, new_cold_accum = adagrad(cold_rows[0], cold_accum[0], cold_grad)
    hot_total = lax.psum(hot_grad, "wide")
    new_hot_rows, new_hot_accum = adagrad(hot_rows[0], hot_accum[0], hot_total)
    return (
        logits,
        new_hot_rows[None],
        new_hot_accum[None],
        new_cold_rows[None],
        new_cold_accum[None],
    )


def solution(mesh):
    return jax.shard_map(
        on_device,
        mesh=mesh,
        in_specs=(
            P(("wide", "grp"), None),
            P("grp", "wide", None),
            P("grp", "wide", None, None),
            P("grp", None, None),
            P("grp", None),
            P("grp", "wide", None),
            P("grp", "wide"),
            P("wide", None),
            P("wide", None),
            P(),
            P(),
            P(("wide", "grp")),
        ),
        out_specs=(
            P(("wide", "grp")),
            P("grp", None, None),
            P("grp", None),
            P("grp", "wide", None),
            P("grp", "wide"),
        ),
        check_vma=False,
    )
```

profile of v0, /device:TPU:1, one launch (start us, length us, event | category | flops | bytes accessed | tf_op | source)
XLA Modules:
  0.0 454.8 jit_solution(17180965123286825865)
XLA Ops:
  7.2 0.7 all-gather.6.cloned.1.call-update
  7.9 1.4 copy.47
  9.3 11.6 %all-to-all-start = ((s32[64,1,16]{2,1,0:T(1,128)}), s32[64,1,16]{2,1,0:T(1,128)S(1)}, u32[]{:S(2)}, u32[]{:S(2)}) async-start(s32[64,1,16]{2,1,0:T(1,128)} %bitcast.14), calls=%async_computation | async-start | bytes 65536 | tf_op jit(solution)/shard_map/all_to_all | solution.py:58
  20.9 1.1 bitcast_convert_fusion.1
  22.0 8.1 %all-to-all-done = s32[64,1,16]{2,1,0:T(1,128)S(1)} async-done(((s32[64,1,16]{2,1,0:T(1,128)}), s32[64,1,16]{2,1,0:T(1,128)S(1)}, u32[]{:S(2)}, u32[]{:S(2)}) %all-to-all-start) | async-done | bytes 4128 | tf_op jit(solution)/shard_map/all_to_all | solution.py:58
  30.2 0.1 copy.48
  30.2 0.1 copy.49
  30.4 0.1 copy.51
  30.4 0.1 reshape.139
  30.5 0.3 copy-done.4
  30.8 3.2 gather_fusion
  34.0 0.9 broadcast_select_fusion
  34.9 4.7 %all-to-all-start.1 = ((bf16[64,16,128]{2,1,0:T(8,128)(2,1)}), bf16[64,16,128]{2,1,0:T(8,128)(2,1)S(1)}, u32[]{:S(2)}, u32[]{:S(2)}) async-start(bf16[64,16,128]{2,1,0:T(8,128)(2,1)} %broadcast_select_fusion), calls=%async_computation.1 | async-start | bytes 524288 | tf_op jit(solution)/shard_map/all_to_all | solution.py:61
  39.7 0.7 all-gather.4.cloned.1.call-update
  40.5 11.6 %all-to-all-done.1 = bf16[64,16,128]{2,1,0:T(8,128)(2,1)S(1)} async-done(((bf16[64,16,128]{2,1,0:T(8,128)(2,1)}), bf16[64,16,128]{2,1,0:T(8,128)(2,1)S(1)}, u32[]{:S(2)}, u32[]{:S(2)}) %all-to-all-start.1) | async-done | bytes 262176 | tf_op jit(solution)/shard_map/all_to_all | solution.py:61
  52.2 28.6 %while.21 = (s32[]{:T(128)}, bf16[2,2,512,128]{3,2,0,1:T(8,128)(2,1)S(1)}, s32[2,2,512,8]{2,1,3,0:T(2,128)S(1)}, bf16[3072,128]{1,0:T(8,128)(2,1)S(1)}, s32[]{:T(128)}) while((s32[]{:T(128)}, bf16[2,2,512,128]{3,2,0,1:T(8,128)(2,1)S(1)}, s32[2,2,512,8]{2,1,3,0:T(2,128)S(1)}, bf16[3072,128]{1,0:T(8,128)(2,1)S(1)}, s32[]{:T(128)}) %tuple.68), condition=%wide.region_1.2_spmd, body=%wide.region_0.1_spmd.sunk | while | flops 906100736 | bytes 1212493 | solution.py:75
  52.3 14.2 %fusion.109 = bf16[2,2,512,128]{3,2,0,1:T(8,128)(2,1)S(1)} fusion(bf16[2,2,512,128]{3,2,0,1:T(8,128)(2,1)S(1)} %get-tuple-element.224, s32[]{:T(128)S(6)} %copy.72, s32[2,512]{1,0:T(2,128)S(1)} %get-tuple-element.198, s32[2,512]{1,0:T(2,128)S(1)} %get-tuple-element.199, s32[2,512]{1,0:T(2,128)S(1)} %get-tuple-element.200, ...), kind=kOutput, calls=%fused_computation.36.clone.1 | convolution fusion | flops 906100736 | bytes 1081348 | tf_op jit(solution)/shard_map/while/body/eval_jaxpr/tbs,se->tbe/dot_general | solution.py:71
  66.5 14.2 %fusion.109 = bf16[2,2,512,128]{3,2,0,1:T(8,128)(2,1)S(1)} fusion(bf16[2,2,512,128]{3,2,0,1:T(8,128)(2,1)S(1)} %get-tuple-element.224, s32[]{:T(128)S(6)} %copy.72, s32[2,512]{1,0:T(2,128)S(1)} %get-tuple-element.198, s32[2,512]{1,0:T(2,128)S(1)} %get-tuple-element.199, s32[2,512]{1,0:T(2,128)S(1)} %get-tuple-element.200, ...), kind=kOutput, calls=%fused_computation.36.clone.1 | convolution fusion | flops 906100736 | bytes 1081348 | tf_op jit(solution)/shard_map/while/body/eval_jaxpr/tbs,se->tbe/dot_general | solution.py:71
  80.8 1.3 copy.54
  82.1 10.0 %all-to-all-start.2 = ((bf16[2,1024,128]{2,0,1:T(2,128)(2,1)}), bf16[2,1024,128]{2,0,1:T(2,128)(2,1)S(1)}, u32[]{:S(2)}, u32[]{:S(2)}) async-start(bf16[2,1024,128]{2,0,1:T(2,128)(2,1)} %copy.54), calls=%async_computation.2 | async-start | bytes 1048576 | tf_op jit(solution)/shard_map/all_to_all | solution.py:77
  92.2 17.9 %all-to-all-done.2 = bf16[2,1024,128]{2,0,1:T(2,128)(2,1)S(1)} async-done(((bf16[2,1024,128]{2,0,1:T(2,128)(2,1)}), bf16[2,1024,128]{2,0,1:T(2,128)(2,1)S(1)}, u32[]{:S(2)}, u32[]{:S(2)}) %all-to-all-start.2) | async-done | bytes 524320 | tf_op jit(solution)/shard_map/all_to_all | solution.py:77
  110.1 0.1 copy.55
  110.3 0.8 copy-done.2
  111.1 2.8 reshape.156
  113.9 70.5 %all-gather.4.cloned.1.call-done = bf16[512,2176]{1,0:T(8,128)(2,1)} async-done(((bf16[8,2176]{1,0:T(8,128)(2,1)}), bf16[512,2176]{1,0:T(8,128)(2,1)}) %all-gather.4.cloned.1.call-update) | async-done | bytes 2228240 | tf_op jit(solution)/shard_map/all_gather | solution.py:89
  184.4 3.0 fusion.86
  187.4 1.1 broadcast_multiply_fusion
  188.5 4.4 fusion.83
  192.9 2.5 bitcast_bitcast_fusion
  195.4 7.1 %all-to-all-start.3 = ((bf16[16,128,128]{2,1,0:T(8,128)(2,1)}), bf16[16,128,128]{2,1,0:T(8,128)(2,1)S(1)}, u32[]{:S(2)}, u32[]{:S(2)}) async-start(bf16[16,128,128]{2,1,0:T(8,128)(2,1)} %bitcast_bitcast_fusion), calls=%async_computation.3 | async-start | bytes 1048576 | tf_op jit(solution)/shard_map/all_to_all | solution.py:105
  202.6 17.9 %all-to-all-done.3 = bf16[16,128,128]{2,1,0:T(8,128)(2,1)S(1)} async-done(((bf16[16,128,128]{2,1,0:T(8,128)(2,1)}), bf16[16,128,128]{2,1,0:T(8,128)(2,1)S(1)}, u32[]{:S(2)}, u32[]{:S(2)}) %all-to-all-start.3) | async-done | bytes 524320 | tf_op jit(solution)/shard_map/all_to_all | solution.py:105
  220.5 24.3 %while.22 = (s32[]{:T(128)}, f32[3072,128]{1,0:T(8,128)S(1)}, s32[2,2,512,8]{2,1,3,0:T(2,128)S(1)}, bf16[2,2,512,128]{3,2,0,1:T(8,128)(2,1)S(1)}, s32[]{:T(128)}, /*index=5*/s32[]{:T(128)}) while((s32[]{:T(128)}, f32[3072,128]{1,0:T(8,128)S(1)}, s32[2,2,512,8]{2,1,3,0:T(2,128)S(1)}, bf16[2,2,512,128]{3,2,0,1:T(8,128)(2,1)S(1)}, ...), condition=%wide.region_4.5_spmd.clone, body=%wide.region_3.4_spmd.clone.sunk | while | flops 906756096 | bytes 3571807 | solution.py:117
  220.7 11.9 %fusion.112 = f32[3072,128]{1,0:T(8,128)S(1)} fusion(s32[2,512]{1,0:T(2,128)S(1)} %get-tuple-element.210, s32[2,512]{1,0:T(2,128)S(1)} %get-tuple-element.211, s32[2,512]{1,0:T(2,128)S(1)} %get-tuple-element.212, s32[2,512]{1,0:T(2,128)S(1)} %get-tuple-element.213, s32[2,512]{1,0:T(2,128)S(1)} %get-tuple-element.214, ...), kind=kOutput, calls=%fused_computation.80.clone.1 | convolution fusion | flops 906756096 | bytes 3440645 | tf_op jit(solution)/shard_map/while/body/eval_jaxpr/tbs,tbe->se/dot_general | solution.py:113
  232.7 11.9 %fusion.112 = f32[3072,128]{1,0:T(8,128)S(1)} fusion(s32[2,512]{1,0:T(2,128)S(1)} %get-tuple-element.210, s32[2,512]{1,0:T(2,128)S(1)} %get-tuple-element.211, s32[2,512]{1,0:T(2,128)S(1)} %get-tuple-element.212, s32[2,512]{1,0:T(2,128)S(1)} %get-tuple-element.213, s32[2,512]{1,0:T(2,128)S(1)} %get-tuple-element.214, ...), kind=kOutput, calls=%fused_computation.80.clone.1 | convolution fusion | flops 906756096 | bytes 3440645 | tf_op jit(solution)/shard_map/while/body/eval_jaxpr/tbs,tbe->se/dot_general | solution.py:113
  244.8 1.0 slice.59
  245.9 0.5 broadcast.111
  246.4 0.7 reduce.3
  247.1 0.1 all_to_all.48
  247.2 0.8 slice.60
  248.0 7.0 %all-to-all-start.4 = ((f32[64,16,128]{2,1,0:T(8,128)}), f32[64,16,128]{2,1,0:T(8,128)S(1)}, u32[]{:S(2)}, u32[]{:S(2)}) async-start(f32[64,16,128]{2,1,0:T(8,128)} %bitcast.36), calls=%async_computation.4 | async-start | bytes 1048576 | tf_op jit(solution)/shard_map/all_to_all | solution.py:122
  255.1 180.4 %all-reduce.2.cloned.1.call-done = f32[2048,128]{1,0:T(8,128)} async-done(((f32[2048,128]{1,0:T(8,128)}), f32[2048,128]{1,0:T(8,128)}) %all-reduce.2.cloned.1.call-update) | async-done | bytes 1048592 | tf_op jit(solution)/shard_map/psum | solution.py:130
  435.5 1.6 multiply_reduce_fusion
  437.1 0.6 add.145
  437.7 2.5 fusion.88
  440.3 6.1 %scatter_custom_fusion = f32[1024,128]{1,0:T(8,128)S(1)} fusion(s32[1024]{0:T(1024)S(1)} %bitcast.146, f32[1024,128]{1,0:T(8,128)S(1)} %bitcast.138, f32[]{:T(128)} %constant.10.clone.1), kind=kCustom, calls=%fused_computation.119 | custom fusion | flops 131072 | bytes 524292 | tf_op jit(solution)/shard_map/scatter-add | solution.py:127
  446.4 0.2 multiply_reduce_fusion.1
  446.7 0.6 add.151
  447.3 1.0 fusion.92
  (57 shorter events, 0.6 us)
Async XLA Ops:
  7.2 33.2 %copy-start.6 = (s32[2,1024,8]{1,2,0:T(8,128)S(1)}, s32[2,1024,8]{1,2,0:T(8,128)}, u32[]{:S(2)}) copy-start(s32[2,1024,8]{1,2,0:T(8,128)} %param.17) | copy-start | bytes 196612
  7.2 33.3 %copy-start = (f32[1,2048,128]{2,1,0:T(8,128)S(1)}, f32[1,2048,128]{2,1,0:T(8,128)}, u32[]{:S(2)}) copy-start(f32[1,2048,128]{2,1,0:T(8,128)} %param.19) | copy-start | bytes 3145732
  7.2 103.9 %all-gather.6.cloned.1.call-start = ((), (), s32[]{:S(2)}) async-start(), calls=%async_computation.7 | async-start | bytes 2662400 | tf_op jit(solution)/shard_map/all_gather | solution.py:88
  9.3 20.8 %all-to-all-start = ((s32[64,1,16]{2,1,0:T(1,128)}), s32[64,1,16]{2,1,0:T(1,128)S(1)}, u32[]{:S(2)}, u32[]{:S(2)}) async-start(s32[64,1,16]{2,1,0:T(1,128)} %bitcast.14), calls=%async_computation | async-start | bytes 65536 | tf_op jit(solution)/shard_map/all_to_all | solution.py:58
  30.2 0.6 copy-start.4
  34.9 17.2 %all-to-all-start.1 = ((bf16[64,16,128]{2,1,0:T(8,128)(2,1)}), bf16[64,16,128]{2,1,0:T(8,128)(2,1)S(1)}, u32[]{:S(2)}, u32[]{:S(2)}) async-start(bf16[64,16,128]{2,1,0:T(8,128)(2,1)} %broadcast_select_fusion), calls=%async_computation.1 | async-start | bytes 524288 | tf_op jit(solution)/shard_map/all_to_all | solution.py:61
  39.6 144.8 %all-gather.4.cloned.1.call-start = ((), (), s32[]{:S(2)}) async-start(), calls=%async_computation.5 | async-start | bytes 2263040 | tf_op jit(solution)/shard_map/all_gather | solution.py:89
  52.2 39.9 %copy-start.11 = (bf16[2176]{0:T(1024)(128)(2,1)S(1)}, bf16[2176]{0:T(1024)(128)(2,1)}, u32[]{:S(2)}) copy-start(bf16[2176]{0:T(1024)(128)(2,1)} %param.26) | copy-start | bytes 13060
  52.2 40.0 %copy-start.7 = (bf16[128,128]{1,0:T(8,128)(2,1)S(1)}, bf16[128,128]{1,0:T(8,128)(2,1)}, u32[]{:S(2)}) copy-start(bf16[128,128]{1,0:T(8,128)(2,1)} %param.16) | copy-start | bytes 98308
  82.1 28.0 %all-to-all-start.2 = ((bf16[2,1024,128]{2,0,1:T(2,128)(2,1)}), bf16[2,1024,128]{2,0,1:T(2,128)(2,1)S(1)}, u32[]{:S(2)}, u32[]{:S(2)}) async-start(bf16[2,1024,128]{2,0,1:T(2,128)(2,1)} %copy.54), calls=%async_computation.2 | async-start | bytes 1048576 | tf_op jit(solution)/shard_map/all_to_all | solution.py:77
  110.3 0.8 copy-start.2
  111.1 73.3 %copy-start.10 = (f32[2176]{0:T(1024)S(1)}, f32[2176]{0:T(1024)}, u32[]{:S(2)}) copy-start(f32[2176]{0:T(1024)} %param.25) | copy-start | bytes 26116
  113.9 73.5 %copy-start.13 = (s32[128]{0:T(128)S(1)}, s32[128]{0:T(128)}, u32[]{:S(2)}) copy-start(s32[128]{0:T(128)} %param.27) | copy-start | bytes 1540
  187.4 5.6 %copy-start.12 = (f32[128]{0:T(128)}, f32[128]{0:T(128)S(1)}, u32[]{:S(2)}) copy-start(f32[128]{0:T(128)S(1)} %get-tuple-element.134) | copy-start | bytes 1540
  195.4 25.1 %all-to-all-start.3 = ((bf16[16,128,128]{2,1,0:T(8,128)(2,1)}), bf16[16,128,128]{2,1,0:T(8,128)(2,1)S(1)}, u32[]{:S(2)}, u32[]{:S(2)}) async-start(bf16[16,128,128]{2,1,0:T(8,128)(2,1)} %bitcast_bitcast_fusion), calls=%async_computation.3 | async-start | bytes 1048576 | tf_op jit(solution)/shard_map/all_to_all | solution.py:105
  202.5 233.0 %all-reduce.2.cloned.1.call-start = ((), (), s32[]{:S(2)}) async-start(), calls=%async_computation.6 | async-start | bytes 2097152 | tf_op jit(solution)/shard_map/psum | solution.py:130
  244.8 1.6 copy-start.5
  245.8 191.2 %copy-start.8 = (f32[1,2048]{1,0:T(1,128)S(1)}, f32[1,2048]{1,0:T(1,128)}, u32[]{:S(2)}) copy-start(f32[1,2048]{1,0:T(1,128)} %param.20) | copy-start | bytes 24580
  245.8 191.9 %copy-start.1 = (f32[1,2048,128]{2,1,0:T(8,128)S(1)}, f32[1,2048,128]{2,1,0:T(8,128)}, u32[]{:S(2)}) copy-start(f32[1,2048,128]{2,1,0:T(8,128)} %param.19) | copy-start | bytes 3145732
  248.0 192.2 %all-to-all-start.4 = ((f32[64,16,128]{2,1,0:T(8,128)}), f32[64,16,128]{2,1,0:T(8,128)S(1)}, u32[]{:S(2)}, u32[]{:S(2)}) async-start(f32[64,16,128]{2,1,0:T(8,128)} %bitcast.36), calls=%async_computation.4 | async-start | bytes 1048576 | tf_op jit(solution)/shard_map/all_to_all | solution.py:122
  255.1 191.6 %copy-start.9 = (f32[1,1024]{1,0:T(1,128)S(1)}, f32[1,1024]{1,0:T(1,128)}, u32[]{:S(2)}) copy-start(f32[1,1024]{1,0:T(1,128)} %param.22) | copy-start | bytes 12292
  255.1 192.2 %copy-start.3 = (f32[1,1024,128]{2,1,0:T(8,128)S(1)}, f32[1,1024,128]{2,1,0:T(8,128)}, u32[]{:S(2)}) copy-start(f32[1,1024,128]{2,1,0:T(8,128)} %param.21) | copy-start | bytes 1572868
Sparse Core Ops, SparseCore 0:
  11.4 89.2 all-gather.5
  103.9 80.4 all-gather.3
  246.0 189.4 all-reduce.1
where the time goes:
time: 456 us; the launch traced here: 455 us
  waiting for transfers between devices  308 us (68%)
  matrix products  59.6 us (13%)
  starting transfers between devices  40.6 us (9%)
  other arithmetic  19.2 us (4%)
  between operations  14.1 us (3%)
  local copies, waits for them, and re-layouts  12.9 us (3%)
    psum x1, waiting for transfers between devices, on_device(): hot_total = lax.psum(hot_grad, 'wide')  180 us
    all_gather x1, waiting for transfers between devices, on_device(): lax.all_gather(cross_up, 'wide', axis=0, tiled=True)  70.5 us
    dot_general x2, matrix products, pool_block(): jnp.einsum('tbs,se->tbe', counts, buffer, preferred_element_type=jnp.floa...  28.5 us
    dot_general x2, matrix products, grad_block(): jnp.einsum('tbs,tbe->se', counts, grad_rows, preferred_element_type=jnp.f...  23.8 us
    all_to_all x1, waiting for transfers between devices, on_device(): lax.all_to_all(pooled_local, 'grp', split_axis=1, concat_axis=0, tiled=True)  17.9 us
    all_to_all x1, waiting for transfers between devices, on_device(): lax.all_to_all(d_pooled, 'grp', split_axis=0, concat_axis=1, tiled=True)  17.9 us
    all_to_all x1, starting transfers between devices, on_device(): lax.all_to_all(cold_offset[0, 0], 'wide', split_axis=0, concat_axis=0, ti...  11.6 us
    all_to_all x1, waiting for transfers between devices, on_device(): lax.all_to_all(picked, 'wide', split_axis=0, concat_axis=0, tiled=True)  11.6 us
  transfers between devices with their start and end apart: 8, of which 6 were waited for; matrix products, arithmetic and copies ran while one was open for 10% of the time, Pallas kernels for 0%

commit v1 on v0

v1 whole, which is shorter than its diff:
```python
import functools

import jax
import jax.numpy as jnp
from jax import lax
from jax.experimental import pallas as pl
from jax.experimental.pallas import tpu as pltpu
from jax.sharding import PartitionSpec as P

LEARN = 0.1
EPSILON = 1e-08
LANES = 128
BF = jnp.bfloat16
F32 = jnp.float32


def wide_shape(n_wide):
    return {64: (4, 8, 2), 8: (2, 2, 2)}[n_wide]


def greet(axis, count, me):
    barrier = pltpu.get_barrier_semaphore()

    def hello(step, carry):
        pl.semaphore_signal(
            barrier, inc=1, device_id={axis: lax.rem(me + step, count)}, device_id_type=pl.DeviceIdType.MESH
        )
        return carry

    lax.fori_loop(1, count, hello, 0)
    pl.semaphore_wait(barrier, count - 1)


def push(src, dst, send_sem, recv_sem, target):
    return pltpu.make_async_remote_copy(
        src_ref=src,
        dst_ref=dst,
        send_sem=send_sem,
        recv_sem=recv_sem,
        device_id=target,
        device_id_type=pl.DeviceIdType.MESH,
    )


def fetch_kernel(
    n_wide, ask_ref, cold_ref, shard_ref,
    fetched_ref, asked_out, gathered_ref,
    asked, cold_bf, picked, columns,
    ask_send, ask_recv, row_send, row_recv, x_send, x_recv, up_send, up_recv, dn_send, dn_recv, sib_send, sib_recv, own_sem,
):
    nx, ny, nc = wide_shape(n_wide)
    me = lax.axis_index("wide")
    core = lax.rem(me, nc)
    y = lax.rem(me // nc, ny)
    x = me // (nc * ny)
    sibling = {"wide": me + 1 - 2 * core}
    greet("wide", n_wide, me)

    def at_wide(x_, y_, c_):
        return {"wide": (x_ * ny + y_) * nc + c_}

    def ask_copy(other):
        return push(ask_ref.at[other], asked.at[me], ask_send.at[other], ask_recv.at[me], {"wide": other})

    def ask_from(other):
        return push(ask_ref.at[me], asked.at[other], ask_send.at[me], ask_recv.at[other], {"wide": other})

    def ask_step(step, carry):
        ask_copy(lax.rem(me + step, n_wide)).start()
        return carry

    lax.fori_loop(1, n_wide, ask_step, 0)
    asked[me] = ask_ref[me]

    own = pltpu.make_async_copy(shard_ref, gathered_ref.at[y, core, x], own_sem)
    own.start()
    x_copies = []
    for step in range(1, nx):
        copy = push(
            shard_ref, gathered_ref.at[y, core, x], x_send.at[step], x_recv.at[step],
            at_wide(lax.rem(x + step, nx), y, core),
        )
        copy.start()
        x_copies.append(copy)

    cold_bf[...] = cold_ref[...].astype(BF)

    own.wait()
    for copy in x_copies:
        copy.wait()
    above, below = lax.rem(y + 1, ny), lax.rem(y + ny - 1, ny)
    n_up, n_dn = ny // 2, (ny - 1) // 2

    def block(row):
        return gathered_ref.at[row, core]

    def up_copy(step):
        row = lax.rem(y + ny - step, ny)
        return push(block(row), block(row), up_send.at[step], up_recv.at[step], at_wide(x, above, core))

    def dn_copy(step):
        row = lax.rem(y + step, ny)
        return push(block(row), block(row), dn_send.at[step], dn_recv.at[step], at_wide(x, below, core))

    def sib_copy(index, row):
        return push(block(row), block(row), sib_send.at[index], sib_recv.at[index], sibling)

    up_copy(0).start()
    if n_dn:
        dn_copy(0).start()
    sib_copy(0, y).start()

    def ask_wait(step, carry):
        ask_from(lax.rem(me + step, n_wide)).wait_recv()
        return carry

    lax.fori_loop(1, n_wide, ask_wait, 0)
    cap = picked.shape[1]
    owned = cold_bf.shape[0]
    per_batch = LANES // cap

    def batch_step(batch, carry):
        spread = jnp.concatenate(
            [jnp.broadcast_to(asked[batch * per_batch + k], (cap, LANES)) for k in range(per_batch)], axis=0
        ).astype(F32)
        lane = lax.broadcasted_iota(jnp.int32, (LANES, LANES), 1)
        row = lax.broadcasted_iota(jnp.int32, (LANES, LANES), 0)
        kept = jnp.where(lane == lax.rem(row, cap), spread, 0.0)
        column = jnp.sum(kept, axis=1, keepdims=True)
        asked_out[pl.ds(batch, 1), :] = jnp.sum(
            jnp.transpose(kept), axis=0, keepdims=True
        ).astype(jnp.int32)
        wanted = column.astype(jnp.int32)
        columns_iota = lax.broadcasted_iota(jnp.int32, (LANES, owned), 1)
        chosen = jnp.where(columns_iota == wanted, 1.0, 0.0).astype(BF)
        rows = jnp.dot(chosen, cold_bf[...], preferred_element_type=F32).astype(BF)
        for k in range(per_batch):
            picked[batch * per_batch + k] = rows[k * cap : (k + 1) * cap]
        return carry

    lax.fori_loop(0, n_wide // per_batch, batch_step, 0)

    def row_copy(other):
        return push(picked.at[other], fetched_ref.at[me], row_send.at[other], row_recv.at[me], {"wide": other})

    def row_from(other):
        return push(picked.at[me], fetched_ref.at[other], row_send.at[me], row_recv.at[other], {"wide": other})

    def row_step(step, carry):
        row_copy(lax.rem(me + step, n_wide)).start()
        return carry

    lax.fori_loop(1, n_wide, row_step, 0)
    fetched_ref[me] = picked[me]

    for step in range(n_up):
        up_copy(step).wait_recv()
        if step + 1 < n_up:
            up_copy(step + 1).start()
        sib_copy(1 + step, lax.rem(y + ny - step - 1, ny)).start()
        if step < n_dn:
            dn_copy(step).wait_recv()
            if step + 1 < n_dn:
                dn_copy(step + 1).start()
            sib_copy(1 + n_up + step, lax.rem(y + step + 1, ny)).start()
    for step in range(n_up):
        up_copy(step).wait_send()
    for step in range(n_dn):
        dn_copy(step).wait_send()
    for index in range(ny):
        sib_copy(index, y).wait()

    def finish(step, carry):
        other = lax.rem(me + step, n_wide)
        ask_copy(other).wait_send()
        row_copy(other).wait_send()
        row_from(other).wait_recv()
        return carry

    lax.fori_loop(1, n_wide, finish, 0)


def cross_kernel(
    n_grp, slots_ref, hot_ref, fetched_ref, dense_ref, down_ref, up_ref, bias_ref, head_ref, labels_ref,
    logits_ref, hot_out, cold_out,
    buffer_t, counts, pooled_out, stacked, gain, d_low, d_out, d_in, slot_grad,
    p_send, p_recv, d_send, d_recv,
):
    me = lax.axis_index("grp")
    hot_count, width = hot_ref.shape
    slot_total = buffer_t.shape[1]
    samples = dense_ref.shape[0]
    his = slot_total // LANES
    words = -(-his // 8)
    pool = slots_ref.shape[1]
    greet("grp", n_grp, me)

    stacked[:, :width] = dense_ref[...]
    for k in range(hot_count // LANES):
        rows = pl.ds(k * LANES, LANES)
        buffer_t[:, k * LANES : (k + 1) * LANES] = jnp.transpose(hot_ref[rows, :]).astype(BF)
    for k in range((slot_total - hot_count) // LANES):
        part = fetched_ref[k * LANES : (k + 1) * LANES, :].astype(F32)
        at = hot_count + k * LANES
        buffer_t[:, at : at + LANES] = jnp.transpose(part).astype(BF)

    def pooled_copy(other):
        return push(
            pooled_out.at[other],
            stacked.at[:, pl.ds(pl.multiple_of(width + 2 * width * me, LANES), 2 * width)],
            p_send.at[other], p_recv.at[me], {"grp": other},
        )

    def pooled_from(other):
        return push(
            pooled_out.at[me],
            stacked.at[:, pl.ds(pl.multiple_of(width + 2 * width * other, LANES), 2 * width)],
            p_send.at[me], p_recv.at[other], {"grp": other},
        )

    def count_chunk(chunk):
        at = pl.ds(pl.multiple_of(chunk * samples, LANES), samples)
        slots = jnp.concatenate([slots_ref[0, :, at], slots_ref[1, :, at]], axis=1)
        low = lax.bitwise_and(slots, LANES - 1)
        high = lax.shift_right_logical(slots, 7)
        unit = lax.shift_left(jnp.ones_like(high), 4 * lax.bitwise_and(high, 7))
        parts = [jnp.where(lax.shift_right_logical(high, 3) == k, unit, 0) for k in range(words)]

        def rows_step(q, carry):
            ids = lax.broadcasted_iota(jnp.int32, (16, 2 * samples), 0) + q * 16
            total = [jnp.zeros((16, 2 * samples), jnp.int32) for _ in range(words)]
            for l in range(pool):
                hit = ids == low[l : l + 1, :]
                for k in range(words):
                    total[k] = total[k] + jnp.where(hit, parts[k][l : l + 1, :], 0)
            for h in range(his):
                digit = lax.bitwise_and(lax.shift_right_logical(total[h // 8], 4 * (h % 8)), 15)
                counts[chunk, pl.ds(pl.multiple_of(h * LANES + q * 16, 16), 16), :] = digit.astype(F32).astype(BF)
            return carry

        lax.fori_loop(0, LANES // 16, rows_step, 0)

    def pool_step(step, carry):
        chunk = lax.rem(me + jnp.where(step == n_grp - 1, 0, step + 1), n_grp)
        count_chunk(chunk)
        pooled_t = jnp.dot(buffer_t[...], counts[chunk], preferred_element_type=F32)
        for t in range(2):
            pooled_out[chunk, :, t * width : (t + 1) * width] = jnp.transpose(
                pooled_t[:, t * samples : (t + 1) * samples]
            ).astype(BF)

        @pl.when(step < n_grp - 1)
        def _():
            pooled_copy(chunk).start()

        return carry

    lax.fori_loop(0, n_grp, pool_step, 0)
    stacked[:, pl.ds(pl.multiple_of(width + 2 * width * me, LANES), 2 * width)] = pooled_out[me]

    def pooled_wait(step, carry):
        other = lax.rem(me + step, n_grp)
        pooled_copy(other).wait_send()
        pooled_from(other).wait_recv()
        return carry

    lax.fori_loop(1, n_grp, pooled_wait, 0)

    low_rank = jnp.dot(stacked[...], down_ref[...], preferred_element_type=F32).astype(BF)
    columns = stacked.shape[1]
    partial = jnp.zeros((samples, LANES), F32)
    for k in range(columns // LANES):
        at = slice(k * LANES, (k + 1) * LANES)
        wide = stacked[:, at].astype(F32)
        part = jnp.dot(low_rank, up_ref[:, at], preferred_element_type=F32) + bias_ref[:, at]
        gain[:, at] = part
        partial = partial + (wide * part + wide) * head_ref[:, at].astype(F32)
    logits = jnp.sum(jnp.transpose(partial), axis=0, keepdims=True)
    logits_ref[...] = logits
    residual = jax.nn.sigmoid(logits) - labels_ref[...].astype(F32)
    residual = jnp.transpose(jnp.broadcast_to(residual, (LANES, samples)))
    low_grad = jnp.zeros((samples, low_rank.shape[1]), F32)
    for k in range(columns // LANES):
        at = slice(k * LANES, (k + 1) * LANES)
        d_crossed = residual * head_ref[:, at].astype(F32)
        d_gain = (d_crossed * stacked[:, at].astype(F32)).astype(BF)
        low_grad = low_grad + lax.dot_general(
            d_gain, up_ref[:, at], (((1,), (1,)), ((), ())), preferred_element_type=F32
        )
    d_low[...] = low_grad.astype(BF)

    def d_copy(other):
        return push(d_out.at[other], d_in.at[me], d_send.at[other], d_recv.at[me], {"grp": other})

    def d_from(other):
        return push(d_out.at[me], d_in.at[other], d_send.at[me], d_recv.at[other], {"grp": other})

    def back_step(step, carry):
        other = lax.rem(me + jnp.where(step == n_grp - 1, 0, step + 1), n_grp)
        at = pl.ds(pl.multiple_of(width + 2 * width * other, LANES), 2 * width)
        back = lax.dot_general(
            d_low[...], down_ref[at, :], (((1,), (1,)), ((), ())), preferred_element_type=F32
        )
        d_crossed = jnp.concatenate([residual, residual], axis=1) * head_ref[:, at].astype(F32)
        d_out[other] = (d_crossed * (gain[:, at] + 1.0) + back).astype(BF)

        @pl.when(step < n_grp - 1)
        def _():
            d_copy(other).start()

        return carry

    lax.fori_loop(0, n_grp, back_step, 0)
    d_in[me] = d_out[me]

    def grad_chunk(chunk, first):
        both = d_in[chunk]
        d_rows = jnp.concatenate([both[:, :width], both[:, width:]], axis=0)
        tile = 4 * LANES if slot_total % (4 * LANES) == 0 else LANES

        def tile_step(i, carry):
            at = pl.ds(pl.multiple_of(i * tile, tile), tile)
            part = jnp.dot(counts[chunk, at, :], d_rows, preferred_element_type=F32)
            slot_grad[at, :] = part if first else slot_grad[at, :] + part
            return carry

        lax.fori_loop(0, slot_total // tile, tile_step, 0)

    grad_chunk(me, True)

    def grad_step(step, carry):
        other = lax.rem(me + n_grp - step, n_grp)
        d_copy(other).wait_send()
        d_from(other).wait_recv()
        grad_chunk(other, False)
        return carry

    lax.fori_loop(1, n_grp, grad_step, 0)
    hot_out[...] = slot_grad[:hot_count, :].astype(BF)
    cold_out[...] = slot_grad[hot_count:, :].astype(BF).reshape(cold_out.shape)


def adagrad_rows(rows_ref, accum_ref, gradient, new_rows_ref, new_accum_ref, at):
    square = jnp.sum(jnp.transpose(gradient * gradient), axis=0, keepdims=True)
    accum = accum_ref[:, at] + square / LANES
    new_accum_ref[:, at] = accum
    scale = jnp.transpose(jnp.broadcast_to(jnp.sqrt(accum) + EPSILON, (LANES, LANES)))
    new_rows_ref[at, :] = rows_ref[at, :] - LEARN * gradient / scale


def update_kernel(
    n_wide, hot_grad, cold_grad, asked_ref, hot_ref, hot_accum, cold_ref, cold_accum,
    new_hot, new_hot_accum, new_cold, new_cold_accum,
    cold_in, pair_in, half, rs_in, total, chosen, cold_sum,
    c_send, c_recv, pair_send, pair_recv, rs_send, rs_recv, ag_send, ag_recv, sib_send, sib_recv,
):
    nx, ny, nc = wide_shape(n_wide)
    chips = nx * ny
    me = lax.axis_index("wide")
    core = lax.rem(me, nc)
    chip = me // nc
    sibling = {"wide": me + 1 - 2 * core}
    hot_count = hot_ref.shape[0]
    per_half = hot_count // 2
    per_chip = per_half // chips
    owned = cold_ref.shape[0]
    greet("wide", n_wide, me)

    def half_at(c):
        return pl.ds(pl.multiple_of(c * per_half, per_half), per_half)

    def chip_at(q):
        return pl.ds(pl.multiple_of(q * per_chip, per_chip), per_chip)

    pair = push(hot_grad.at[half_at(1 - core)], pair_in, pair_send, pair_recv, sibling)
    pair.start()

    def cold_copy(other):
        return push(cold_grad.at[other], cold_in.at[me], c_send.at[other], c_recv.at[me], {"wide": other})

    def cold_from(other):
        return push(cold_grad.at[me], cold_in.at[other], c_send.at[me], c_recv.at[other], {"wide": other})

    def cold_step(step, carry):
        cold_copy(lax.rem(me + step, n_wide)).start()
        return carry

    lax.fori_loop(1, n_wide, cold_step, 0)
    cold_in[me] = cold_grad[me]

    pair.wait()
    half[...] = (hot_grad[half_at(core), :].astype(F32) + pair_in[...].astype(F32)).astype(BF)

    def rs_copy(q):
        return push(
            half.at[chip_at(q)], rs_in.at[chip], rs_send.at[q], rs_recv.at[chip], {"wide": q * nc + core}
        )

    def rs_from(q):
        return push(
            half.at[chip_at(q)], rs_in.at[q], rs_send.at[q], rs_recv.at[q], {"wide": q * nc + core}
        )

    def rs_step(step, carry):
        rs_copy(lax.rem(chip + step, chips)).start()
        return carry

    lax.fori_loop(1, chips, rs_step, 0)
    rs_in[chip] = half[chip_at(chip), :]

    def fill(batch, carry):
        ids = lax.broadcasted_iota(jnp.int32, (owned, LANES), 0)
        chosen[:, pl.ds(pl.multiple_of(batch * LANES, LANES), LANES)] = jnp.where(
            ids == asked_ref[pl.ds(batch, 1), :], 1.0, 0.0
        ).astype(BF)
        return carry

    lax.fori_loop(0, chosen.shape[1] // LANES, fill, 0)

    def cold_wait(step, carry):
        other = lax.rem(me + step, n_wide)
        cold_from(other).wait_recv()
        cold_copy(other).wait_send()
        return carry

    lax.fori_loop(1, n_wide, cold_wait, 0)
    arrived = cold_in[...].reshape(chosen.shape[1], LANES)
    cold_sum[...] = jnp.dot(chosen[...], arrived, preferred_element_type=F32)

    def cold_update(i, carry):
        at = pl.ds(pl.multiple_of(i * LANES, LANES), LANES)
        adagrad_rows(cold_ref, cold_accum, cold_sum[at, :], new_cold, new_cold_accum, at)
        return carry

    lax.fori_loop(0, owned // LANES, cold_update, 0)

    def rs_wait(step, carry):
        q = lax.rem(chip + step, chips)
        rs_from(q).wait_recv()
        rs_copy(q).wait_send()
        return carry

    lax.fori_loop(1, chips, rs_wait, 0)

    def own_at(c, q):
        return pl.ds(pl.multiple_of(c * per_half + q * per_chip, per_chip), per_chip)

    def add(q, so_far):
        return so_far + rs_in[q].astype(F32)

    summed = lax.fori_loop(0, chips, add, jnp.zeros((per_chip, LANES), F32))
    total[own_at(core, chip), :] = summed.astype(BF)

    def ag_copy(q):
        return push(
            total.at[own_at(core, chip)], total.at[own_at(core, chip)], ag_send.at[q], ag_recv.at[chip],
            {"wide": q * nc + core},
        )

    def ag_from(q):
        return push(
            total.at[own_at(core, q)], total.at[own_at(core, q)], ag_send.at[q], ag_recv.at[q],
            {"wide": q * nc + core},
        )

    def ag_step(step, carry):
        ag_copy(lax.rem(chip + step, chips)).start()
        return carry

    lax.fori_loop(1, chips, ag_step, 0)

    def ag_wait(step, carry):
        q = lax.rem(chip + step, chips)
        ag_from(q).wait_recv()
        ag_copy(q).wait_send()
        return carry

    lax.fori_loop(1, chips, ag_wait, 0)
    sib = push(total.at[half_at(core)], total.at[half_at(core)], sib_send, sib_recv, sibling)
    sib.start()

    def hot_update(c):
        def step(i, carry):
            at = pl.ds(pl.multiple_of(c * per_half + i * LANES, LANES), LANES)
            adagrad_rows(hot_ref, hot_accum, total[at, :].astype(F32), new_hot, new_hot_accum, at)
            return carry

        lax.fori_loop(0, per_half // LANES, step, 0)

    hot_update(core)
    sib.wait()
    hot_update(1 - core)


VMEM = pl.BlockSpec(memory_space=pltpu.VMEM)
ANY = pl.BlockSpec(memory_space=pl.ANY)
DMA = pltpu.SemaphoreType.DMA


def params(collective_id):
    return pltpu.CompilerParams(
        collective_id=collective_id, has_side_effects=True, vmem_limit_bytes=56 * 1024 * 1024
    )


def on_device(
    n_wide, n_grp,
    dense_features, bag_slots, cold_offset, hot_rows, hot_accum, cold_rows, cold_accum,
    cross_down, cross_up, cross_bias, out_weight, labels,
):
    nx, ny, nc = wide_shape(n_wide)
    samples, width = dense_features.shape
    hot_count = hot_rows.shape[1]
    owned = cold_rows.shape[1]
    cap = cold_offset.shape[3]
    requests = n_wide * cap
    slot_total = hot_count + requests
    down_rows, rank = cross_down.shape
    up_rows, columns = cross_up.shape
    down_size, up_size = (down_rows * rank // LANES, up_rows * columns // LANES)
    shard = jnp.concatenate(
        [
            cross_down.reshape(down_rows, rank // LANES, LANES).transpose(1, 0, 2).reshape(down_size, LANES),
            cross_up.reshape(up_rows, columns // LANES, LANES).transpose(1, 0, 2).reshape(up_size, LANES),
        ]
    )
    ask = jnp.pad(cold_offset[0, 0], ((0, 0), (0, LANES - cap))).reshape(n_wide, 1, LANES)
    fetched, asked, gathered = pl.pallas_call(
        functools.partial(fetch_kernel, n_wide),
        out_shape=(
            jax.ShapeDtypeStruct((n_wide, cap, width), BF),
            jax.ShapeDtypeStruct((requests // LANES, LANES), jnp.int32),
            jax.ShapeDtypeStruct((ny, nc, nx) + shard.shape, BF),
        ),
        in_specs=[VMEM, VMEM, ANY],
        out_specs=(VMEM, VMEM, ANY),
        scratch_shapes=[
            pltpu.VMEM((n_wide, 1, LANES), jnp.int32),
            pltpu.VMEM((owned, width), BF),
            pltpu.VMEM((n_wide, cap, width), BF),
            pltpu.VMEM((LANES, LANES), F32),
            DMA((n_wide,)), DMA((n_wide,)), DMA((n_wide,)), DMA((n_wide,)),
            DMA((nx,)), DMA((nx,)), DMA((ny,)), DMA((ny,)), DMA((ny,)), DMA((ny,)), DMA((ny,)), DMA((ny,)),
            DMA,
        ],
        compiler_params=params(0),
        name="fetch_and_gather",
    )(ask, cold_rows[0], shard)

    ordered = gathered.transpose(2, 0, 1, 3, 4).reshape(n_wide, down_size + up_size, LANES)
    down_full = (
        ordered[:, :down_size].reshape(n_wide, rank // LANES, down_rows, LANES)
        .transpose(0, 2, 1, 3).reshape(n_wide * down_rows, rank)
    )
    up_full = (
        ordered[:, down_size:].reshape(n_wide, columns // LANES, up_rows, LANES)
        .transpose(0, 2, 1, 3).reshape(n_wide * up_rows, columns)
    )

    slots = jnp.transpose(bag_slots, (0, 2, 1))
    logits, hot_grad, cold_grad = pl.pallas_call(
        functools.partial(cross_kernel, n_grp),
        out_shape=(
            jax.ShapeDtypeStruct((1, samples), F32),
            jax.ShapeDtypeStruct((hot_count, width), BF),
            jax.ShapeDtypeStruct((n_wide, cap, width), BF),
        ),
        in_specs=[VMEM] * 9,
        out_specs=(VMEM, VMEM, VMEM),
        scratch_shapes=[
            pltpu.VMEM((width, slot_total), BF),
            pltpu.VMEM((n_grp, slot_total, 2 * samples), BF),
            pltpu.VMEM((n_grp, samples, 2 * width), BF),
            pltpu.VMEM((samples, columns), BF),
            pltpu.VMEM((samples, columns), F32),
            pltpu.VMEM((samples, rank), BF),
            pltpu.VMEM((n_grp, samples, 2 * width), BF),
            pltpu.VMEM((n_grp, samples, 2 * width), BF),
            pltpu.VMEM((slot_total, width), F32),
            DMA((n_grp,)), DMA((n_grp,)), DMA((n_grp,)), DMA((n_grp,)),
        ],
        compiler_params=params(1),
        name="pool_cross_grad",
    )(
        slots, hot_rows[0], fetched.reshape(requests, width), dense_features, down_full, up_full,
        cross_bias.reshape(1, columns), out_weight.reshape(1, columns), labels.reshape(1, samples),
    )

    chips = nx * ny
    per_chip = hot_count // 2 // chips
    new_hot, new_hot_accum, new_cold, new_cold_accum = pl.pallas_call(
        functools.partial(update_kernel, n_wide),
        out_shape=(
            jax.ShapeDtypeStruct((hot_count, width), F32),
            jax.ShapeDtypeStruct((1, hot_count), F32),
            jax.ShapeDtypeStruct((owned, width), F32),
            jax.ShapeDtypeStruct((1, owned), F32),
        ),
        in_specs=[VMEM] * 7,
        out_specs=(VMEM,) * 4,
        scratch_shapes=[
            pltpu.VMEM((n_wide, cap, width), BF),
            pltpu.VMEM((hot_count // 2, width), BF),
            pltpu.VMEM((hot_count // 2, width), BF),
            pltpu.VMEM((chips, per_chip, width), BF),
            pltpu.VMEM((hot_count, width), BF),
            pltpu.VMEM((owned, requests), BF),
            pltpu.VMEM((owned, width), F32),
            DMA((n_wide,)), DMA((n_wide,)), DMA, DMA,
            DMA((chips,)), DMA((chips,)), DMA((chips,)), DMA((chips,)), DMA, DMA,
        ],
        compiler_params=params(2),
        name="exchange_and_update",
    )(hot_grad, cold_grad, asked, hot_rows[0], hot_accum, cold_rows[0], cold_accum)
    return (logits.reshape(samples), new_hot[None], new_hot_accum, new_cold[None], new_cold_accum)


def solution(mesh):
    return jax.shard_map(
        functools.partial(on_device, mesh.shape["wide"], mesh.shape["grp"]),
        mesh=mesh,
        in_specs=(
            P(("wide", "grp"), None),
            P("grp", "wide", None),
            P("grp", "wide", None, None),
            P("grp", None, None),
            P("grp", None),
            P("grp", "wide", None),
            P("grp", "wide"),
            P("wide", None),
            P("wide", None),
            P(),
            P(),
            P(("wide", "grp")),
        ),
        out_specs=(
            P(("wide", "grp")),
            P("grp", None, None),
            P("grp", None),
            P("grp", "wide", None),
            P("grp", "wide"),
        ),
        check_vma=False,
    )
```

time: 456 us -> 172 us (0.38)
  waiting for transfers between devices: 308 us -> 0 us
  Pallas kernels: 0 us -> 152 us
  matrix products: 59.6 us -> 0 us
  starting transfers between devices: 40.6 us -> 0 us
  other arithmetic: 19.2 us -> 1.4 us
  between operations: 14.1 us -> 0.75 us
    psum x1 -> x0, waiting for transfers between devices: 180 us -> none  [on_device(): hot_total = lax.psum(hot_grad, 'wide')]
    pallas_call x0 -> x3, Pallas kernels: none -> 152 us  [the longest x1 59.6 us: on_device(): pl.pallas_call(functools.partial(fetch_kernel, n_wide), out_shape=(jax.Sh...]
    all_gather x2 -> x0, waiting for transfers between devices: 70.5 us -> none  [the longest x1 70.5 us: on_device(): lax.all_gather(cross_up, 'wide', axis=0, tiled=True)]
    dot_general x6 -> x0, matrix products: 59.6 us -> none  [the longest x2 28.5 us: pool_block(): jnp.einsum('tbs,se->tbe', counts, buffer, preferred_element_type=jnp.floa...]
    all_to_all x5 -> x0, waiting for transfers between devices: 55.6 us -> none  [the longest x1 17.9 us: on_device(): lax.all_to_all(pooled_local, 'grp', split_axis=1, concat_axis=0, tiled=True)]
    all_to_all x5 -> x0, starting transfers between devices: 40.5 us -> none  [the longest x1 11.6 us: on_device(): lax.all_to_all(cold_offset[0, 0], 'wide', split_axis=0, concat_axis=0, ti...]
    scatter-add x1 -> x0, other arithmetic: 6.14 us -> none  [on_device(): cold_grad = jnp.zeros((owned_rows, row_width), jnp.float32).at[target.res...]
  transfers between devices with their start and end apart: 8 -> 0, of which waited for: 6 -> 0; matrix products, arithmetic and copies ran while one was open for 10% -> 0% of each run, Pallas kernels for 0% -> 0%
where the time goes in v1:
time: 172 us
  Pallas kernels  152 us (88%)
  local copies, waits for them, and re-layouts  17.3 us (10%)
    pallas_call x1, Pallas kernels, on_device(): pl.pallas_call(functools.partial(fetch_kernel, n_wide), out_shape=(jax.Sh...  59.6 us
    pallas_call x1, Pallas kernels, on_device(): pl.pallas_call(functools.partial(cross_kernel, n_grp), out_shape=(jax.Sha...  52.1 us
    pallas_call x1, Pallas kernels, on_device(): pl.pallas_call(functools.partial(update_kernel, n_wide), out_shape=(jax.S...  40.5 us
    unnamed x17, local copies, waits for them, and re-layouts  7.99 us

profile of v1, /device:TPU:1, one launch (start us, length us, event | category | flops | bytes accessed | tf_op | source)
XLA Modules:
  0.0 171.6 jit_solution(9881929808334989472)
XLA Ops:
  0.6 0.8 reshape.56
  1.5 1.4 pad_maximum_fusion.shard_ref
  2.9 0.8 copy.19
  3.7 0.6 pad.4
  4.3 59.6 %fetch_and_gather.1 = (bf16[64,16,128]{2,1,0:T(8,128)(2,1)}, s32[8,128]{1,0:T(8,128)}, bf16[8,2,4,272,128]{4,3,2,1,0:T(8,128)(2,1)}) custom-call(s32[64,1,128]{2,1,0:T(1,128)} %bitcast.47, f32[1024,128]{1,0:T(8,128)} %bitcast.41, bf16[272,128]{1,0:T(8,128)(2,1)} %pad_maximum_fusion.shard_ref), custom_call_target="tpu_custom_call" | custom-call | tf_op jit(solution)/shard_map/fetch_and_gather/pallas_call | solution.py:528
  63.9 2.6 %copy.21 = bf16[4,8,2,272,128]{4,3,2,1,0:T(8,128)(2,1)S(1)} copy(bf16[4,8,2,272,128]{4,3,0,2,1:T(8,128)(2,1)} %bitcast.38) | data formatting | bytes 8912896 | tf_op jit(solution)/shard_map/transpose | solution.py:550
  66.5 1.7 slice_bitcast_fusion
  68.2 0.6 copy.22
  68.8 1.7 %copy.23 = bf16[64,34,4,128]{3,2,1,0:T(4,128)(2,1)S(1)} copy(bf16[64,34,4,128]{3,0,1,2:T(8,128)(2,1)S(1)} %bitcast.36) | data formatting | bytes 4456448 | tf_op jit(solution)/shard_map/transpose | solution.py:553
  70.5 0.0 copy-start.1
  70.5 0.0 copy-start.2
  70.5 1.7 %copy.27 = bf16[272,8,4,128]{3,1,2,0:T(8,128)(2,1)} copy(bf16[272,8,4,128]{3,2,1,0:T(4,128)(2,1)S(1)} %bitcast.37) | data formatting | bytes 4456448
  72.3 0.0 copy-done.1
  72.3 0.6 reshape.66.bias_ref
  72.9 0.0 copy-done.2
  72.9 0.6 reshape.67.head_ref
  73.5 52.1 %pool_cross_grad.1 = (f32[1,128]{1,0:T(1,128)}, bf16[2048,128]{1,0:T(8,128)(2,1)}, bf16[64,16,128]{2,1,0:T(8,128)(2,1)}) custom-call(s32[2,8,1024]{2,1,0:T(8,128)} %bitcast.49, f32[2048,128]{1,0:T(8,128)} %bitcast.39, bf16[1024,128]{1,0:T(8,128)(2,1)} %bitcast.45, bf16[128,128]{1,0:T(8,128)(2,1)} %dense_ref.1, bf16[2176,512]{1,0:T(8,128)(2,1)} %bitcast.35, ...), custom_call_target="tpu_custom_call" | custom-call | tf_op jit(solution)/shard_map/pool_cross_grad/pallas_call | solution.py:561
  125.5 0.0 copy-start.4
  125.6 40.5 %exchange_and_update.1 = (f32[2048,128]{1,0:T(8,128)}, f32[1,2048]{1,0:T(1,128)}, f32[1024,128]{1,0:T(8,128)}, f32[1,1024]{1,0:T(1,128)}) custom-call(bf16[2048,128]{1,0:T(8,128)(2,1)} %get-tuple-element.18.hot_grad, bf16[64,16,128]{2,1,0:T(8,128)(2,1)} %get-tuple-element.19.cold_grad, s32[8,128]{1,0:T(8,128)} %get-tuple-element.20.asked_ref, ...), custom_call_target="tpu_custom_call" | custom-call | tf_op jit(solution)/shard_map/exchange_and_update/pallas_call | solution.py:591
  166.1 0.0 copy-start
  166.1 0.0 copy-start.3
  166.1 0.0 copy-done.4
  166.1 0.5 copy.34
  166.6 2.3 %copy.35 = f32[1,2048,128]{2,1,0:T(8,128)} copy(f32[1,2048,128]{2,1,0:T(8,128)} %bitcast.43) | data formatting | bytes 2097152
  168.9 1.3 copy.36
  170.2 0.0 copy-done
  170.2 0.8 copy.37
  171.0 0.0 copy-done.3
  171.0 0.6 copy.38
  (2 shorter events, 0.0 us)
Async XLA Ops:
  70.5 1.8 %copy-start.1 = (f32[2176]{0:T(1024)S(1)}, f32[2176]{0:T(1024)}, u32[]{:S(2)}) copy-start(f32[2176]{0:T(1024)} %param.21) | copy-start | bytes 26116
  70.5 2.4 %copy-start.2 = (bf16[2176]{0:T(1024)(128)(2,1)S(1)}, bf16[2176]{0:T(1024)(128)(2,1)}, u32[]{:S(2)}) copy-start(bf16[2176]{0:T(1024)(128)(2,1)} %param.22) | copy-start | bytes 13060
  125.5 40.5 %copy-start.4 = (f32[1,128]{1,0:T(1,128)S(1)}, f32[1,128]{1,0:T(1,128)}, u32[]{:S(2)}) copy-start(f32[1,128]{1,0:T(1,128)} %get-tuple-element.17) | copy-start | bytes 1540
  166.1 4.1 %copy-start = (f32[1024,128]{1,0:T(8,128)S(1)}, f32[1024,128]{1,0:T(8,128)}, u32[]{:S(2)}) copy-start(f32[1024,128]{1,0:T(8,128)} %get-tuple-element.23) | copy-start | bytes 1572868
  166.1 4.9 %copy-start.3 = (f32[1,1024]{1,0:T(1,128)S(1)}, f32[1,1024]{1,0:T(1,128)}, u32[]{:S(2)}) copy-start(f32[1,1024]{1,0:T(1,128)} %get-tuple-element.36) | copy-start | bytes 12292

commit v2 on v0

v2 whole, which is shorter than its diff:
```python
import functools

import jax
import jax.numpy as jnp
from jax import lax
from jax.experimental import pallas as pl
from jax.experimental.pallas import tpu as pltpu
from jax.sharding import PartitionSpec as P

LEARN = 0.1
EPSILON = 1e-08
LANES = 128
BF = jnp.bfloat16
F32 = jnp.float32


def wide_shape(n_wide):
    return {64: (4, 8, 2), 8: (2, 2, 2)}[n_wide]


def round_up(value, unit):
    return -(-value // unit) * unit


def push(src, dst, send_sem, recv_sem, target):
    return pltpu.make_async_remote_copy(
        src_ref=src,
        dst_ref=dst,
        send_sem=send_sem,
        recv_sem=recv_sem,
        device_id=target,
        device_id_type=pl.DeviceIdType.MESH,
    )


def each(first, last, body):
    def step(i, carry):
        body(i)
        return carry

    lax.fori_loop(first, last, step, 0)


def far_first(count):
    return sorted(range(1, count), key=lambda o: -min(o, count - o)) + [0]


def step_kernel(
    n_wide, n_grp,
    offset_ref, cold_ref, down_ref, up_ref, slots_ref, hot_ref, dense_ref, small_ref,
    logits_ref, total_ref, cold_sum_ref,
    ask, asked, asked_lane, cold_bf, picked, fetched,
    shard32, shard_down, shard_up, all_down, all_up, down32, down, up,
    buffer_t, counts, pooled_hot, pooled_out, stacked, gain, d_low, d_out, d_in, slot_grad,
    hot_grad, cold_grad, cold_in, pair_in, half, rs_in, chosen,
    ask_send, ask_recv, row_send, row_recv,
    d1_send, d1_recv, d_up_send, d_up_recv, d_dn_send, d_dn_recv, d_sib_send, d_sib_recv,
    u1_send, u1_recv, u_up_send, u_up_recv, u_dn_send, u_dn_recv, u_sib_send, u_sib_recv,
    p_send, p_recv, g_send, g_recv,
    c_send, c_recv, pair_send, pair_recv, rs_send, rs_recv, ag_send, ag_recv, sib_send, sib_recv,
):
    nx, ny, nc = wide_shape(n_wide)
    chips = nx * ny
    me = lax.axis_index("wide")
    grp = lax.axis_index("grp")
    core = lax.rem(me, nc)
    chip = me // nc
    y = lax.rem(chip, ny)
    x = chip // ny
    sibling = {"wide": me + 1 - 2 * core}
    hot_count, width = hot_ref.shape
    owned = cold_ref.shape[0]
    cap = picked.shape[1]
    slot_total = buffer_t.shape[1]
    samples = dense_ref.shape[0]
    columns = stacked.shape[1]
    his = slot_total // LANES
    words = -(-his // 8)
    pool = slots_ref.shape[1]
    order = far_first(n_grp)

    def at_wide(x_, y_):
        return {"wide": (x_ * ny + y_) * nc + core}

    barrier = pltpu.get_barrier_semaphore()
    for axis, count, mine in (("wide", n_wide, me), ("grp", n_grp, grp)):
        each(1, count, lambda step: pl.semaphore_signal(
            barrier, inc=1, device_id={axis: lax.rem(mine + step, count)}, device_id_type=pl.DeviceIdType.MESH
        ))

    ask[...] = jnp.zeros_like(ask)
    for other in range(n_wide):
        ask[other, :, :cap] = offset_ref[other : other + 1, :]
    down_rows, rank = down_ref.shape
    up_rows = up_ref.shape[0]
    shard32[...] = jnp.zeros_like(shard32)
    for j in range(rank // LANES):
        shard32[j * down_rows : (j + 1) * down_rows, :] = down_ref[:, j * LANES : (j + 1) * LANES].astype(F32)
    shard_down[...] = shard32[...].astype(BF)
    for j in range(columns // LANES):
        shard32[j * up_rows : (j + 1) * up_rows, :] = up_ref[:, j * LANES : (j + 1) * LANES].astype(F32)
    shard_up[...] = shard32[...].astype(BF)
    all_down[y, core, x] = shard_down[...]
    all_up[x, core, y] = shard_up[...]
    pl.semaphore_wait(barrier, n_wide + n_grp - 2)

    def ask_copy(other):
        return push(ask.at[other], asked.at[me], ask_send.at[other], ask_recv.at[me], {"wide": other})

    def ask_from(other):
        return push(ask.at[me], asked.at[other], ask_send.at[me], ask_recv.at[other], {"wide": other})

    each(1, n_wide, lambda step: ask_copy(lax.rem(me + step, n_wide)).start())
    asked[me] = ask[me]

    def down_first(step):
        return push(
            shard_down, all_down.at[y, core, x], d1_send.at[step], d1_recv.at[step], at_wide(lax.rem(x + step, nx), y)
        )

    def up_first(step):
        return push(
            shard_up, all_up.at[x, core, y], u1_send.at[step], u1_recv.at[step], at_wide(x, lax.rem(y + step, ny))
        )

    for step in far_first(nx)[:-1]:
        down_first(step).start()
    for step in far_first(ny)[:-1]:
        up_first(step).start()

    def ring(blocks, mine, length, place, sems):
        fwd_send, fwd_recv, bwd_send, bwd_recv, side_send, side_recv = sems
        n_fwd, n_bwd = length // 2, (length - 1) // 2

        def block(index):
            return blocks.at[index, core]

        def fwd(step):
            held = block(lax.rem(mine + length - step, length))
            return push(held, held, fwd_send.at[step], fwd_recv.at[step], place(lax.rem(mine + 1, length)))

        def bwd(step):
            held = block(lax.rem(mine + step, length))
            return push(held, held, bwd_send.at[step], bwd_recv.at[step], place(lax.rem(mine + length - 1, length)))

        def side(step):
            held = block(lax.rem(mine + length - step, length))
            return push(held, held, side_send.at[step], side_recv.at[step], sibling)

        def start():
            fwd(0).start()
            if n_bwd:
                bwd(0).start()
            side(0).start()

        def serve(step):
            fwd(step).wait_recv()
            if step + 1 < n_fwd:
                fwd(step + 1).start()
            side(step + 1).start()
            if step < n_bwd:
                bwd(step).wait_recv()
                if step + 1 < n_bwd:
                    bwd(step + 1).start()
                side(length - step - 1).start()

        def drain():
            for step in range(n_fwd):
                fwd(step).wait_send()
            for step in range(n_bwd):
                bwd(step).wait_send()
            for step in range(length):
                side(step).wait()

        return start, [functools.partial(serve, step) for step in range(n_fwd)], drain

    down_start, down_serve, down_drain = ring(
        all_down, y, ny, lambda row: at_wide(x, row),
        (d_up_send, d_up_recv, d_dn_send, d_dn_recv, d_sib_send, d_sib_recv),
    )
    up_start, up_serve, up_drain = ring(
        all_up, x, nx, lambda row: at_wide(row, y),
        (u_up_send, u_up_recv, u_dn_send, u_dn_recv, u_sib_send, u_sib_recv),
    )

    def weights_second():
        for step in range(1, nx):
            down_first(step).wait()
        down_start()
        for step in range(1, ny):
            up_first(step).wait()
        up_start()

    def count_chunk(chunk):
        at = pl.ds(pl.multiple_of(chunk * samples, LANES), samples)
        slots = jnp.concatenate([slots_ref[0, :, at], slots_ref[1, :, at]], axis=1)
        low = lax.bitwise_and(slots, LANES - 1)
        high = lax.shift_right_logical(slots, 7)
        unit = lax.shift_left(jnp.ones_like(high), 4 * lax.bitwise_and(high, 7))
        parts = [jnp.where(lax.shift_right_logical(high, 3) == k, unit, 0) for k in range(words)]

        def rows_step(q):
            ids = lax.broadcasted_iota(jnp.int32, (16, 2 * samples), 0) + q * 16
            total = [jnp.zeros((16, 2 * samples), jnp.int32) for _ in range(words)]
            for l in range(pool):
                hit = ids == low[l : l + 1, :]
                for k in range(words):
                    total[k] = total[k] + jnp.where(hit, parts[k][l : l + 1, :], 0)
            for h in range(his):
                digit = lax.bitwise_and(lax.shift_right_logical(total[h // 8], 4 * (h % 8)), 15)
                counts[chunk, pl.ds(pl.multiple_of(h * LANES + q * 16, 16), 16), :] = digit.astype(F32).astype(BF)

        each(0, LANES // 16, rows_step)

    def chunk_of(index):
        return lax.rem(grp + order[index], n_grp)

    def hot_pool(chunk):
        pooled_hot[chunk] = jnp.dot(
            buffer_t[:, :hot_count], counts[chunk, :hot_count, :], preferred_element_type=F32
        )

    early = (3 * n_grp) // 8
    for index in range(early):
        count_chunk(chunk_of(index))
    weights_second()
    cold_bf[...] = cold_ref[...].astype(BF)

    each(1, n_wide, lambda step: ask_from(lax.rem(me + step, n_wide)).wait_recv())
    per_batch = LANES // cap

    def batch_step(batch):
        spread = jnp.concatenate(
            [jnp.broadcast_to(asked[batch * per_batch + k], (cap, LANES)) for k in range(per_batch)], axis=0
        ).astype(F32)
        lane = lax.broadcasted_iota(jnp.int32, (LANES, LANES), 1)
        row = lax.broadcasted_iota(jnp.int32, (LANES, LANES), 0)
        kept = jnp.where(lane == lax.rem(row, cap), spread, 0.0)
        wanted = jnp.sum(kept, axis=1, keepdims=True).astype(jnp.int32)
        asked_lane[pl.ds(batch, 1), :] = jnp.sum(jnp.transpose(kept), axis=0, keepdims=True).astype(jnp.int32)
        hit = lax.broadcasted_iota(jnp.int32, (LANES, owned), 1) == wanted
        rows = jnp.dot(jnp.where(hit, 1.0, 0.0).astype(BF), cold_bf[...], preferred_element_type=F32).astype(BF)
        for k in range(per_batch):
            picked[batch * per_batch + k] = rows[k * cap : (k + 1) * cap]

    each(0, n_wide // per_batch, batch_step)

    def row_copy(other):
        return push(picked.at[other], fetched.at[me], row_send.at[other], row_recv.at[me], {"wide": other})

    def row_from(other):
        return push(picked.at[me], fetched.at[other], row_send.at[me], row_recv.at[other], {"wide": other})

    each(1, n_wide, lambda step: row_copy(lax.rem(me + step, n_wide)).start())
    fetched[me] = picked[me]

    stacked[:, :width] = dense_ref[...]
    for k in range(hot_count // LANES):
        buffer_t[:, k * LANES : (k + 1) * LANES] = jnp.transpose(hot_ref[k * LANES : (k + 1) * LANES, :]).astype(BF)
    serve = [list(down_serve), list(up_serve)]

    def serve_next(which):
        if serve[which]:
            serve[which].pop(0)()

    for index in range(n_grp):
        chunk = chunk_of(index)
        if index >= early:
            count_chunk(chunk)
        hot_pool(chunk)
        if index == n_grp // 2:
            serve_next(0)
    serve_next(1)
    serve_next(0)

    def fill(batch):
        ids = lax.broadcasted_iota(jnp.int32, (owned, LANES), 0)
        chosen[:, pl.ds(pl.multiple_of(batch * LANES, LANES), LANES)] = jnp.where(
            ids == asked_lane[pl.ds(batch, 1), :], 1.0, 0.0
        ).astype(BF)

    each(0, chosen.shape[1] // LANES, fill)

    def row_wait(step):
        other = lax.rem(me + step, n_wide)
        row_from(other).wait_recv()
        row_copy(other).wait_send()
        ask_copy(other).wait_send()

    each(1, n_wide, row_wait)
    for k in range((slot_total - hot_count) // LANES):
        part = jnp.concatenate([fetched[k * per_batch + i] for i in range(per_batch)], axis=0).astype(F32)
        at = hot_count + k * LANES
        buffer_t[:, at : at + LANES] = jnp.transpose(part).astype(BF)

    def table_lanes(owner):
        return pl.ds(pl.multiple_of(width + 2 * width * owner, LANES), 2 * width)

    def pooled_copy(other):
        return push(pooled_out.at[other], stacked.at[:, table_lanes(grp)], p_send.at[other], p_recv.at[grp], {"grp": other})

    def pooled_from(other):
        return push(pooled_out.at[grp], stacked.at[:, table_lanes(other)], p_send.at[grp], p_recv.at[other], {"grp": other})

    for index in range(n_grp):
        chunk = chunk_of(index)
        pooled_t = pooled_hot[chunk] + jnp.dot(
            buffer_t[:, hot_count:], counts[chunk, hot_count:, :], preferred_element_type=F32
        )
        for t in range(2):
            pooled_out[chunk, :, t * width : (t + 1) * width] = jnp.transpose(
                pooled_t[:, t * samples : (t + 1) * samples]
            ).astype(BF)
        if index < n_grp - 1:
            pooled_copy(chunk).start()
    stacked[:, table_lanes(grp)] = pooled_out[grp]

    while serve[0] or serve[1]:
        serve_next(0)
        serve_next(1)
    down_drain()
    up_drain()
    down_size = rank // LANES * down_rows

    def down_shard(w):
        shard32[...] = all_down[lax.rem(w // nc, ny), lax.rem(w, nc), w // (nc * ny)].astype(F32)
        for j in range(rank // LANES):
            down32[j, pl.ds(w * down_rows, down_rows), :] = shard32[j * down_rows : (j + 1) * down_rows, :]

    each(0, n_wide, down_shard)

    def down_round(i):
        at = pl.ds(pl.multiple_of(i * LANES, LANES), LANES)
        for j in range(rank // LANES):
            down[at, j * LANES : (j + 1) * LANES] = down32[j, at, :].astype(BF)

    each(0, columns // LANES, down_round)

    def up_shard(q):
        both = [all_up[q // ny, c, lax.rem(q, ny)].astype(F32) for c in range(nc)]
        for j in range(columns // LANES):
            up[pl.ds(pl.multiple_of(q * nc * up_rows, nc * up_rows), nc * up_rows), j * LANES : (j + 1) * LANES] = (
                jnp.concatenate([part[j * up_rows : (j + 1) * up_rows] for part in both], axis=0).astype(BF)
            )

    each(0, chips, up_shard)

    for index in range(n_grp - 1):
        pooled_copy(chunk_of(index)).wait_send()
        pooled_from(lax.rem(grp + n_grp - order[index], n_grp)).wait_recv()

    def bias_at(at):
        return small_ref[:, at]

    def head_at(start, size):
        if isinstance(start, int):
            return small_ref[:, columns + start : columns + start + size]
        return small_ref[:, pl.ds(pl.multiple_of(columns + start, LANES), size)]

    low_rank = jnp.dot(stacked[...], down[...], preferred_element_type=F32).astype(BF)
    partial = jnp.zeros((samples, LANES), F32)
    for k in range(columns // LANES):
        at = slice(k * LANES, (k + 1) * LANES)
        wide = stacked[:, at].astype(F32)
        part = jnp.dot(low_rank, up[:, at], preferred_element_type=F32) + bias_at(at)
        gain[:, at] = part
        partial = partial + (wide * part + wide) * head_at(k * LANES, LANES)
    logits = jnp.sum(jnp.transpose(partial), axis=0, keepdims=True)
    logits_ref[...] = logits
    residual = jax.nn.sigmoid(logits) - small_ref[:, 2 * columns :]
    residual = jnp.transpose(jnp.broadcast_to(residual, (LANES, samples)))
    low_grad = jnp.zeros((samples, rank), F32)
    for k in range(columns // LANES):
        at = slice(k * LANES, (k + 1) * LANES)
        d_crossed = residual * head_at(k * LANES, LANES)
        d_gain = (d_crossed * stacked[:, at].astype(F32)).astype(BF)
        low_grad = low_grad + lax.dot_general(
            d_gain, up[:, at], (((1,), (1,)), ((), ())), preferred_element_type=F32
        )
    d_low[...] = low_grad.astype(BF)

    def d_copy(other):
        return push(d_out.at[other], d_in.at[grp], g_send.at[other], g_recv.at[grp], {"grp": other})

    def d_from(other):
        return push(d_out.at[grp], d_in.at[other], g_send.at[grp], g_recv.at[other], {"grp": other})

    for index in range(n_grp):
        other = chunk_of(index)
        at = table_lanes(other)
        back = lax.dot_general(
            d_low[...], down[at, :], (((1,), (1,)), ((), ())), preferred_element_type=F32
        )
        d_crossed = jnp.concatenate([residual, residual], axis=1) * head_at(width + 2 * width * other, 2 * width)
        d_out[other] = (d_crossed * (gain[:, at] + 1.0) + back).astype(BF)
        if index < n_grp - 1:
            d_copy(other).start()
    d_in[grp] = d_out[grp]

    tile = 4 * LANES if slot_total % (4 * LANES) == 0 else LANES

    def grad_chunk(chunk, first, last):
        both = d_in[chunk]
        d_rows = jnp.concatenate([both[:, :width], both[:, width:]], axis=0)

        def tile_step(i):
            at = pl.ds(pl.multiple_of(i * tile, tile), tile)
            part = jnp.dot(counts[chunk, at, :], d_rows, preferred_element_type=F32)
            slot_grad[at, :] = part if first else slot_grad[at, :] + part

        each(0, slot_total // tile, tile_step)

    grad_chunk(grp, True, n_grp == 1)
    for index in range(n_grp - 1):
        other = lax.rem(grp + n_grp - order[index], n_grp)
        d_copy(chunk_of(index)).wait_send()
        d_from(other).wait_recv()
        grad_chunk(other, False, index == n_grp - 2)
    hot_grad[...] = slot_grad[:hot_count, :].astype(BF)
    cold_grad[...] = slot_grad[hot_count:, :].astype(BF).reshape(cold_grad.shape)

    per_half = hot_count // 2
    per_chip = per_half // chips

    def half_at(c):
        return pl.ds(pl.multiple_of(c * per_half, per_half), per_half)

    def chip_at(q):
        return pl.ds(pl.multiple_of(q * per_chip, per_chip), per_chip)

    pair = push(hot_grad.at[half_at(1 - core)], pair_in, pair_send, pair_recv, sibling)
    pair.start()

    def cold_copy(other):
        return push(cold_grad.at[other], cold_in.at[me], c_send.at[other], c_recv.at[me], {"wide": other})

    def cold_from(other):
        return push(cold_grad.at[me], cold_in.at[other], c_send.at[me], c_recv.at[other], {"wide": other})

    def rs_copy(q):
        return push(half.at[chip_at(q)], rs_in.at[chip], rs_send.at[q], rs_recv.at[chip], {"wide": q * nc + core})

    def rs_from(q):
        return push(half.at[chip_at(q)], rs_in.at[q], rs_send.at[q], rs_recv.at[q], {"wide": q * nc + core})

    pair.wait()
    half[...] = (hot_grad[half_at(core), :].astype(F32) + pair_in[...].astype(F32)).astype(BF)
    each(1, chips, lambda step: rs_copy(lax.rem(chip + step, chips)).start())
    rs_in[chip] = half[chip_at(chip), :]
    each(1, n_wide, lambda step: cold_copy(lax.rem(me + step, n_wide)).start())
    cold_in[me] = cold_grad[me]

    def rs_wait(step):
        q = lax.rem(chip + step, chips)
        rs_from(q).wait_recv()
        rs_copy(q).wait_send()

    each(1, chips, rs_wait)

    def own_at(q):
        return pl.ds(pl.multiple_of(core * per_half + q * per_chip, per_chip), per_chip)

    summed = lax.fori_loop(
        0, chips, lambda q, so_far: so_far + rs_in[q].astype(F32), jnp.zeros((per_chip, LANES), F32)
    )
    total_ref[own_at(chip), :] = summed.astype(BF)

    def ag_copy(q):
        mine = total_ref.at[own_at(chip)]
        return push(mine, mine, ag_send.at[q], ag_recv.at[chip], {"wide": q * nc + core})

    def ag_from(q):
        theirs = total_ref.at[own_at(q)]
        return push(theirs, theirs, ag_send.at[q], ag_recv.at[q], {"wide": q * nc + core})

    each(1, chips, lambda step: ag_copy(lax.rem(chip + step, chips)).start())

    def cold_wait(step):
        other = lax.rem(me + step, n_wide)
        cold_from(other).wait_recv()
        cold_copy(other).wait_send()

    each(1, n_wide, cold_wait)
    cold_sum_ref[...] = jnp.dot(
        chosen[...], cold_in[...].reshape(chosen.shape[1], LANES), preferred_element_type=F32
    )

    def ag_wait(step):
        q = lax.rem(chip + step, chips)
        ag_from(q).wait_recv()
        ag_copy(q).wait_send()

    each(1, chips, ag_wait)
    side = push(total_ref.at[half_at(core)], total_ref.at[half_at(core)], sib_send, sib_recv, sibling)
    side.start()
    side.wait()


def adagrad_kernel(
    logits_in, hot_grad, cold_grad, hot_ref, hot_accum, cold_ref, cold_accum,
    logits_ref, new_hot, new_hot_accum, new_cold, new_cold_accum,
):
    logits_ref[...] = logits_in[...]
    for grad_ref, rows_ref, accum_ref, new_rows, new_accum in (
        (hot_grad, hot_ref, hot_accum, new_hot, new_hot_accum),
        (cold_grad, cold_ref, cold_accum, new_cold, new_cold_accum),
    ):
        for start in range(0, rows_ref.shape[0], LANES):
            at = slice(start, start + LANES)
            gradient = grad_ref[at, :].astype(F32)
            square = jnp.sum(jnp.transpose(gradient * gradient), axis=0, keepdims=True)
            accum = accum_ref[:, at] + square / LANES
            new_accum[:, at] = accum
            scale = jnp.transpose(jnp.broadcast_to(jnp.sqrt(accum) + EPSILON, (LANES, LANES)))
            new_rows[at, :] = rows_ref[at, :] - LEARN * gradient / scale


VMEM = pl.BlockSpec(memory_space=pltpu.VMEM)
DMA = pltpu.SemaphoreType.DMA


def on_device(
    n_wide, n_grp,
    dense_features, bag_slots, cold_offset, hot_rows, hot_accum, cold_rows, cold_accum,
    cross_down, cross_up, cross_bias, out_weight, labels,
):
    nx, ny, nc = wide_shape(n_wide)
    chips = nx * ny
    samples, width = dense_features.shape
    hot_count = hot_rows.shape[1]
    owned = cold_rows.shape[1]
    cap = cold_offset.shape[3]
    requests = n_wide * cap
    slot_total = hot_count + requests
    down_rows, rank = cross_down.shape
    up_rows, columns = cross_up.shape
    shard_rows = round_up(max(down_rows * rank, up_rows * columns) // LANES, 16)
    slots = jnp.transpose(bag_slots, (0, 2, 1))
    small = jnp.concatenate([cross_bias, out_weight.astype(F32), labels.astype(F32)]).reshape(1, -1)

    def vm(*shape, dtype=BF):
        return pltpu.VMEM(shape, dtype)

    logits, hot_grad, cold_grad = pl.pallas_call(
        functools.partial(step_kernel, n_wide, n_grp),
        out_shape=(
            jax.ShapeDtypeStruct((1, samples), F32),
            jax.ShapeDtypeStruct((hot_count, width), BF),
            jax.ShapeDtypeStruct((owned, width), F32),
        ),
        in_specs=[VMEM] * 8,
        out_specs=(VMEM,) * 3,
        scratch_shapes=[
            vm(n_wide, 1, LANES, dtype=jnp.int32), vm(n_wide, 1, LANES, dtype=jnp.int32),
            vm(requests // LANES, LANES, dtype=jnp.int32),
            vm(owned, width), vm(n_wide, cap, width), vm(n_wide, cap, width),
            vm(shard_rows, LANES, dtype=F32), vm(shard_rows, LANES), vm(shard_rows, LANES),
            vm(ny, nc, nx, shard_rows, LANES), vm(nx, nc, ny, shard_rows, LANES),
            vm(rank // LANES, columns, LANES, dtype=F32), vm(columns, rank), vm(rank, columns),
            vm(width, slot_total), vm(n_grp, slot_total, 2 * samples),
            vm(n_grp, width, 2 * samples, dtype=F32), vm(n_grp, samples, 2 * width),
            vm(samples, columns), vm(samples, columns, dtype=F32), vm(samples, rank),
            vm(n_grp, samples, 2 * width), vm(n_grp, samples, 2 * width), vm(slot_total, width, dtype=F32),
            vm(hot_count, width), vm(n_wide, cap, width), vm(n_wide, cap, width),
            vm(hot_count // 2, width), vm(hot_count // 2, width), vm(chips, hot_count // 2 // chips, width),
            vm(owned, requests),
            DMA((n_wide,)), DMA((n_wide,)), DMA((n_wide,)), DMA((n_wide,)),
            DMA((nx,)), DMA((nx,)), DMA((ny,)), DMA((ny,)), DMA((ny,)), DMA((ny,)), DMA((ny,)), DMA((ny,)),
            DMA((ny,)), DMA((ny,)), DMA((nx,)), DMA((nx,)), DMA((nx,)), DMA((nx,)), DMA((nx,)), DMA((nx,)),
            DMA((n_grp,)), DMA((n_grp,)), DMA((n_grp,)), DMA((n_grp,)),
            DMA((n_wide,)), DMA((n_wide,)), DMA, DMA,
            DMA((chips,)), DMA((chips,)), DMA((chips,)), DMA((chips,)), DMA, DMA,
        ],
        compiler_params=pltpu.CompilerParams(
            collective_id=0, has_side_effects=True, vmem_limit_bytes=60 * 1024 * 1024
        ),
        name="train_step",
    )(cold_offset[0, 0], cold_rows[0], cross_down, cross_up, slots, hot_rows[0], dense_features, small)

    steps = 8 if hot_count % (8 * LANES) == 0 and owned % (8 * LANES) == 0 else 1
    hot_block, cold_block = hot_count // steps, owned // steps

    def rows_spec(size):
        return pl.BlockSpec((size, width), lambda i: (i, 0))

    def accum_spec(size):
        return pl.BlockSpec((1, size), lambda i: (0, i))

    whole = pl.BlockSpec((1, samples), lambda i: (0, 0))
    logits, new_hot, new_hot_accum, new_cold, new_cold_accum = pl.pallas_call(
        adagrad_kernel,
        grid=(steps,),
        out_shape=(
            jax.ShapeDtypeStruct((1, samples), F32),
            jax.ShapeDtypeStruct((hot_count, width), F32),
            jax.ShapeDtypeStruct((1, hot_count), F32),
            jax.ShapeDtypeStruct((owned, width), F32),
            jax.ShapeDtypeStruct((1, owned), F32),
        ),
        in_specs=[
            whole, rows_spec(hot_block), rows_spec(cold_block),
            rows_spec(hot_block), accum_spec(hot_block), rows_spec(cold_block), accum_spec(cold_block),
        ],
        out_specs=(whole, rows_spec(hot_block), accum_spec(hot_block), rows_spec(cold_block), accum_spec(cold_block)),
        name="adagrad",
    )(logits, hot_grad, cold_grad, hot_rows[0], hot_accum, cold_rows[0], cold_accum)
    return (logits.reshape(samples), new_hot[None], new_hot_accum, new_cold[None], new_cold_accum)


def solution(mesh):
    return jax.shard_map(
        functools.partial(on_device, mesh.shape["wide"], mesh.shape["grp"]),
        mesh=mesh,
        in_specs=(
            P(("wide", "grp"), None),
            P("grp", "wide", None),
            P("grp", "wide", None, None),
            P("grp", None, None),
            P("grp", None),
            P("grp", "wide", None),
            P("grp", "wide"),
            P("wide", None),
            P("wide", None),
            P(),
            P(),
            P(("wide", "grp")),
        ),
        out_specs=(
            P(("wide", "grp")),
            P("grp", None, None),
            P("grp", None),
            P("grp", "wide", None),
            P("grp", "wide"),
        ),
        check_vma=False,
    )
```

time: 456 us -> 118 us (0.26)
  waiting for transfers between devices: 308 us -> 0 us
  Pallas kernels: 0 us -> 115 us
  matrix products: 59.6 us -> 0 us
  starting transfers between devices: 40.6 us -> 0 us
  other arithmetic: 19.2 us -> 0.68 us
  between operations: 14.1 us -> 0.67 us
  local copies, waits for them, and re-layouts: 12.9 us -> 1.42 us
    psum x1 -> x0, waiting for transfers between devices: 180 us -> none  [on_device(): hot_total = lax.psum(hot_grad, 'wide')]
    pallas_call x0 -> x2, Pallas kernels: none -> 115 us  [the longest x1 109 us: on_device(): pl.pallas_call(functools.partial(step_kernel, n_wide, n_grp), out_shape=(...]
    all_gather x2 -> x0, waiting for transfers between devices: 70.5 us -> none  [the longest x1 70.5 us: on_device(): lax.all_gather(cross_up, 'wide', axis=0, tiled=True)]
    dot_general x6 -> x0, matrix products: 59.6 us -> none  [the longest x2 28.5 us: pool_block(): jnp.einsum('tbs,se->tbe', counts, buffer, preferred_element_type=jnp.floa...]
    all_to_all x5 -> x0, waiting for transfers between devices: 55.6 us -> none  [the longest x1 17.9 us: on_device(): lax.all_to_all(pooled_local, 'grp', split_axis=1, concat_axis=0, tiled=True)]
    all_to_all x5 -> x0, starting transfers between devices: 40.5 us -> none  [the longest x1 11.6 us: on_device(): lax.all_to_all(cold_offset[0, 0], 'wide', split_axis=0, concat_axis=0, ti...]
    scatter-add x1 -> x0, other arithmetic: 6.14 us -> none  [on_device(): cold_grad = jnp.zeros((owned_rows, row_width), jnp.float32).at[target.res...]
  transfers between devices with their start and end apart: 8 -> 0, of which waited for: 6 -> 0; matrix products, arithmetic and copies ran while one was open for 10% -> 0% of each run, Pallas kernels for 0% -> 0%
where the time goes in v2:
time: 118 us
  Pallas kernels  115 us (97%)
  local copies, waits for them, and re-layouts  1.42 us (1%)
    pallas_call x1, Pallas kernels, on_device(): pl.pallas_call(functools.partial(step_kernel, n_wide, n_grp), out_shape=(...  109 us
    pallas_call x1, Pallas kernels, on_device(): pl.pallas_call(adagrad_kernel, grid=(steps,), out_shape=(jax.ShapeDtypeSt...  6.52 us

profile of v2, /device:TPU:1, one launch (start us, length us, event | category | flops | bytes accessed | tf_op | source)
XLA Modules:
  0.0 118.0 jit_solution(8798711087303920141)
XLA Ops:
  0.6 0.0 copy-start.2
  0.6 0.0 copy-start
  0.7 0.7 convert_element_type.7
  1.3 0.0 copy-done.2
  1.3 0.0 copy-done
  1.4 0.0 copy-start.1
  1.4 0.6 reshape.16.small_ref
  2.0 0.1 copy-done.1
  2.1 0.7 copy.17
  2.8 108.7 %train_step.1 = (f32[1,128]{1,0:T(1,128)}, bf16[2048,128]{1,0:T(8,128)(2,1)}, f32[1024,128]{1,0:T(8,128)}) custom-call(s32[64,16]{1,0:T(8,128)} %bitcast.11, f32[1024,128]{1,0:T(8,128)} %bitcast.9, bf16[34,512]{1,0:T(8,128)(2,1)} %down_ref.1, bf16[8,2176]{1,0:T(8,128)(2,1)} %up_ref.1, s32[2,8,1024]{2,1,0:T(8,128)} %bitcast.12, f32[2048,128]{1,0:T(8,128)} %bitcast.7, ...), custom_call_target="tpu_custom_call" | custom-call | tf_op jit(solution)/shard_map/train_step/pallas_call | solution.py:544
  111.4 6.5 %adagrad.1 = (f32[1,128]{1,0:T(1,128)}, f32[2048,128]{1,0:T(8,128)}, f32[1,2048]{1,0:T(1,128)}, f32[1024,128]{1,0:T(8,128)}, f32[1,1024]{1,0:T(1,128)}) custom-call(f32[1,128]{1,0:T(1,128)} %get-tuple-element.13.logits_in, bf16[2048,128]{1,0:T(8,128)(2,1)} %get-tuple-element.14.hot_grad, f32[1024,128]{1,0:T(8,128)} %get-tuple-element.15.cold_grad, ...), custom_call_target="tpu_custom_call" | custom-call | tf_op jit(solution)/shard_map/adagrad/pallas_call | solution.py:590
  (2 shorter events, 0.0 us)
Async XLA Ops:
  0.6 0.7 copy-start.2
  0.6 0.7 copy-start
  1.4 0.7 copy-start.1

commit v3 on v2

v3 whole, which is shorter than its diff:
```python
import functools

import jax
import jax.numpy as jnp
from jax import lax
from jax.experimental import pallas as pl
from jax.experimental.pallas import tpu as pltpu
from jax.sharding import PartitionSpec as P

LEARN = 0.1
EPSILON = 1e-08
LANES = 128
GRADIENT_TILE = 1024
GRADIENT_PARTS = {8: [(7, 8), (0, 3), (3, 7)], 2: [(1, 2), (0, 1)]}
BF = jnp.bfloat16
F32 = jnp.float32


def wide_shape(n_wide):
    return {64: (4, 8, 2), 8: (2, 2, 2)}[n_wide]


def round_up(value, unit):
    return -(-value // unit) * unit


def push(src, dst, send_sem, recv_sem, target):
    return pltpu.make_async_remote_copy(
        src_ref=src,
        dst_ref=dst,
        send_sem=send_sem,
        recv_sem=recv_sem,
        device_id=target,
        device_id_type=pl.DeviceIdType.MESH,
    )


def each(first, last, body):
    def step(i, carry):
        body(i)
        return carry

    lax.fori_loop(first, last, step, 0)


def far_first(count):
    return sorted(range(1, count), key=lambda o: -min(o, count - o)) + [0]


def step_kernel(
    n_wide, n_grp,
    offset_ref, cold_hbm, down_ref, up_ref, slots_ref, hot_hbm, dense_ref, bias_ref, head_ref, labels_ref,
    logits_ref, total_ref, cold_sum_ref,
    cold_ref, hot_ref, small, square, ask, asked, asked_lane, cold_bf, picked, fetched,
    shard32, shard_down, shard_up, all_down, all_up, down32, down, up,
    buffer_t, counts, pooled_hot, pooled_out, stacked, gain, d_low, d_out, d_in, slot_grad,
    hot_grad, cold_grad, cold_in, pair_in, half, x_in, quarter, y_in, chosen,
    load_sem, ask_sem, row_sem, d1_sem, u1_sem, p_sem, c_sem, pair_sem, xrs_sem, yrs_sem, yag_sem,
    d_send, d_fwd, d_bwd, d_side, u_send, u_fwd, u_bwd, u_side, g_send, g_recv, xag_send, xag_recv, sib_send, sib_recv,
):
    nx, ny, nc = wide_shape(n_wide)
    chips = nx * ny
    me = lax.axis_index("wide")
    grp = lax.axis_index("grp")
    core = lax.rem(me, nc)
    chip = me // nc
    y = lax.rem(chip, ny)
    x = chip // ny
    sibling = {"wide": me + 1 - 2 * core}
    hot_count, width = hot_ref.shape
    owned = cold_ref.shape[0]
    cap = picked.shape[1]
    slot_total = buffer_t.shape[1]
    samples = dense_ref.shape[0]
    columns = stacked.shape[1]
    his = slot_total // LANES
    words = -(-his // 8)
    pool = slots_ref.shape[1]
    order = far_first(n_grp)

    def at_wide(x_, y_):
        return {"wide": (x_ * ny + y_) * nc + core}

    def bytes_of(ref, sems):
        return push(ref, ref, sems.at[0], sems.at[1], sibling)

    loads = [
        pltpu.make_async_copy(cold_hbm, cold_ref, load_sem.at[0]),
        pltpu.make_async_copy(hot_hbm, hot_ref, load_sem.at[1]),
    ]
    for load in loads:
        load.start()

    barrier = pltpu.get_barrier_semaphore()
    for axis, count, mine in (("wide", n_wide, me), ("grp", n_grp, grp)):
        each(1, count, lambda step: pl.semaphore_signal(
            barrier, inc=1, device_id={axis: lax.rem(mine + step, count)}, device_id_type=pl.DeviceIdType.MESH
        ))

    square[...] = jnp.zeros_like(square)
    square[:cap, :n_wide] = offset_ref[...].astype(F32)
    ask[...] = jnp.transpose(square[...])[:n_wide]
    for k in range(columns // LANES):
        at = slice(k * LANES, (k + 1) * LANES)
        small[:, at] = bias_ref[at].reshape(1, LANES)
        small[:, columns + k * LANES : columns + (k + 1) * LANES] = head_ref[at].astype(F32).reshape(1, LANES)
    small[:, 2 * columns :] = labels_ref[...].astype(F32).reshape(1, samples)
    down_rows, rank = down_ref.shape
    up_rows = up_ref.shape[0]
    shard32[...] = jnp.zeros_like(shard32)
    for j in range(rank // LANES):
        shard32[j * down_rows : (j + 1) * down_rows, :] = down_ref[:, j * LANES : (j + 1) * LANES].astype(F32)
    shard_down[...] = shard32[...].astype(BF)
    for j in range(columns // LANES):
        shard32[j * up_rows : (j + 1) * up_rows, :] = up_ref[:, j * LANES : (j + 1) * LANES].astype(F32)
    shard_up[...] = shard32[...].astype(BF)
    all_down[y, core, x] = shard_down[...]
    all_up[x, core, y] = shard_up[...]
    pl.semaphore_wait(barrier, n_wide + n_grp - 2)

    def row_of(index):
        return pl.ds(index, 1)

    def ask_copy(other):
        return push(ask.at[row_of(other)], asked.at[row_of(me)], ask_sem.at[0], ask_sem.at[1], {"wide": other})

    each(1, n_wide, lambda step: ask_copy(lax.rem(me + step, n_wide)).start())
    asked[row_of(me), :] = ask[row_of(me), :]

    for step in far_first(nx)[:-1]:
        push(
            shard_down, all_down.at[y, core, x], d1_sem.at[0], d1_sem.at[1], at_wide(lax.rem(x + step, nx), y)
        ).start()
    for step in far_first(ny)[:-1]:
        push(
            shard_up, all_up.at[x, core, y], u1_sem.at[0], u1_sem.at[1], at_wide(x, lax.rem(y + step, ny))
        ).start()

    def ring(blocks, mine, length, place, send, fwd_recv, bwd_recv, side_recv):
        n_fwd, n_bwd = length // 2, (length - 1) // 2

        def index(step):
            return lax.rem(mine + length - step, length)

        def fwd(step):
            held = blocks.at[index(step), core]
            return push(held, held, send.at[0], fwd_recv.at[step], place(lax.rem(mine + 1, length)))

        def bwd(step):
            held = blocks.at[lax.rem(mine + step, length), core]
            return push(held, held, send.at[1], bwd_recv.at[step], place(lax.rem(mine + length - 1, length)))

        def side(step):
            held = blocks.at[index(step), core]
            return push(held, held, send.at[2], side_recv.at[step], sibling)

        def start():
            fwd(0).start()
            if n_bwd:
                bwd(0).start()
            side(0).start()

        def serve(step):
            fwd(step).wait_recv()
            if step + 1 < n_fwd:
                fwd(step + 1).start()
            side(step + 1).start()
            if step < n_bwd:
                bwd(step).wait_recv()
                if step + 1 < n_bwd:
                    bwd(step + 1).start()
                side(length - step - 1).start()

        def ready(step):
            side(step).wait_recv()
            return index(step)

        def drain():
            for which, count in enumerate((n_fwd, n_bwd, length)):
                if count:
                    held = blocks.at[pl.ds(0, count), core]
                    push(held, held, send.at[which], side_recv.at[0], sibling).wait_send()

        steps = [[0]] + [[step + 1] + ([length - step - 1] if step < n_bwd else []) for step in range(n_fwd)]
        return start, serve, ready, drain, steps

    down_start, down_serve, down_ready, down_drain, down_steps = ring(
        all_down, y, ny, lambda row: at_wide(x, row), d_send, d_fwd, d_bwd, d_side
    )
    up_start, up_serve, up_ready, up_drain, up_steps = ring(
        all_up, x, nx, lambda row: at_wide(row, y), u_send, u_fwd, u_bwd, u_side
    )

    def down_rows_of(row):
        def shard(i):
            x_, c = i // nc, lax.rem(i, nc)
            shard32[...] = all_down[row, c, x_].astype(F32)
            first = ((x_ * ny + row) * nc + c) * down_rows
            for j in range(rank // LANES):
                down32[j, pl.ds(first, down_rows), :] = shard32[j * down_rows : (j + 1) * down_rows, :]

        each(0, nx * nc, shard)

    def up_rows_of(x_):
        def pair_of(y_):
            both = [all_up[x_, c, y_].astype(F32) for c in range(nc)]
            first = pl.multiple_of((x_ * ny + y_) * nc * up_rows, nc * up_rows)
            for j in range(columns // LANES):
                up[pl.ds(first, nc * up_rows), j * LANES : (j + 1) * LANES] = jnp.concatenate(
                    [part[j * up_rows : (j + 1) * up_rows] for part in both], axis=0
                ).astype(BF)

        each(0, ny, pair_of)

    def serve_down(step):
        if step < len(down_steps) - 1:
            down_serve(step)

    def serve_up(step):
        if step < len(up_steps) - 1:
            up_serve(step)

    def lay_down(step):
        for block in down_steps[step] if step < len(down_steps) else []:
            down_rows_of(down_ready(block))

    def lay_up(step):
        for block in up_steps[step] if step < len(up_steps) else []:
            up_rows_of(up_ready(block))

    def chunk_of(index):
        return lax.rem(grp + order[index], n_grp)

    def lanes_of(first, last):
        return slice(first * 2 * samples, last * 2 * samples)

    def count_chunk(index):
        chunk = chunk_of(index)
        at = pl.ds(pl.multiple_of(chunk * samples, LANES), samples)
        slots = jnp.concatenate([slots_ref[0, :, at], slots_ref[1, :, at]], axis=1)
        low = lax.bitwise_and(slots, LANES - 1)
        high = lax.shift_right_logical(slots, 7)
        unit = lax.shift_left(jnp.ones_like(high), 4 * lax.bitwise_and(high, 7))
        parts = [jnp.where(lax.shift_right_logical(high, 3) == k, unit, 0) for k in range(words)]

        def rows_step(q):
            ids = lax.broadcasted_iota(jnp.int32, (16, 2 * samples), 0) + q * 16
            total = [jnp.zeros((16, 2 * samples), jnp.int32) for _ in range(words)]
            for l in range(pool):
                hit = ids == low[l : l + 1, :]
                for k in range(words):
                    total[k] = total[k] + jnp.where(hit, parts[k][l : l + 1, :], 0)
            for h in range(his):
                digit = lax.bitwise_and(lax.shift_right_logical(total[h // 8], 4 * (h % 8)), 15)
                counts[pl.ds(pl.multiple_of(h * LANES + q * 16, 16), 16), lanes_of(index, index + 1)] = digit.astype(F32).astype(BF)

        each(0, LANES // 16, rows_step)

    def hot_pool(index):
        pooled_hot[index] = jnp.dot(
            buffer_t[:, :hot_count], counts[:hot_count, lanes_of(index, index + 1)], preferred_element_type=F32
        )

    early = (3 * n_grp) // 8
    for index in range(early):
        count_chunk(index)
    loads[0].wait()
    cold_bf[...] = cold_ref[...].astype(BF)
    bytes_of(all_down.at[y, core, pl.ds(0, nx - 1)], d1_sem).wait()
    down_start()

    asks = bytes_of(ask.at[pl.ds(0, n_wide - 1)], ask_sem)
    asks.wait_recv()
    per_batch = LANES // cap

    batches = n_wide // per_batch

    def batch_step(step):
        batch = lax.rem(me // per_batch + step, batches)
        spread = jnp.concatenate(
            [jnp.broadcast_to(asked[row_of(batch * per_batch + k), :], (cap, LANES)) for k in range(per_batch)], axis=0
        )
        lane = lax.broadcasted_iota(jnp.int32, (LANES, LANES), 1)
        row = lax.broadcasted_iota(jnp.int32, (LANES, LANES), 0)
        kept = jnp.where(lane == lax.rem(row, cap), spread, 0.0)
        wanted = jnp.sum(kept, axis=1, keepdims=True).astype(jnp.int32)
        asked_lane[pl.ds(batch, 1), :] = jnp.sum(jnp.transpose(kept), axis=0, keepdims=True).astype(jnp.int32)
        hit = lax.broadcasted_iota(jnp.int32, (LANES, owned), 1) == wanted
        rows = jnp.dot(jnp.where(hit, 1.0, 0.0).astype(BF), cold_bf[...], preferred_element_type=F32).astype(BF)
        for k in range(per_batch):
            other = batch * per_batch + k
            picked[other] = rows[k * cap : (k + 1) * cap]

            @pl.when(other != me)
            def _():
                push(
                    picked.at[other], fetched.at[me], row_sem.at[0], row_sem.at[1], {"wide": other}
                ).start()

    each(0, batches, batch_step)
    fetched[me] = picked[me]
    bytes_of(all_up.at[x, core, pl.ds(0, ny - 1)], u1_sem).wait()
    up_start()
    serve_down(0)

    stacked[:, :width] = dense_ref[...]
    loads[1].wait()
    for k in range(hot_count // LANES):
        buffer_t[:, k * LANES : (k + 1) * LANES] = jnp.transpose(hot_ref[k * LANES : (k + 1) * LANES, :]).astype(BF)
    for index in range(n_grp):
        if index >= early:
            count_chunk(index)
        hot_pool(index)

    def fill(batch):
        ids = lax.broadcasted_iota(jnp.int32, (owned, LANES), 0)
        chosen[:, pl.ds(pl.multiple_of(batch * LANES, LANES), LANES)] = jnp.where(
            ids == asked_lane[pl.ds(batch, 1), :], 1.0, 0.0
        ).astype(BF)

    asks.wait_send()
    rows_moved = bytes_of(picked.at[pl.ds(0, n_wide - 1)], row_sem)
    rows_moved.wait_recv()
    for k in range((slot_total - hot_count) // LANES):
        part = jnp.concatenate([fetched[k * per_batch + i] for i in range(per_batch)], axis=0).astype(F32)
        at = hot_count + k * LANES
        buffer_t[:, at : at + LANES] = jnp.transpose(part).astype(BF)

    def table_lanes(owner):
        return pl.ds(pl.multiple_of(width + 2 * width * owner, LANES), 2 * width)

    for index in range(n_grp):
        chunk = chunk_of(index)
        pooled_t = pooled_hot[index] + jnp.dot(
            buffer_t[:, hot_count:], counts[hot_count:, lanes_of(index, index + 1)], preferred_element_type=F32
        )
        for t in range(2):
            pooled_out[chunk, :, t * width : (t + 1) * width] = jnp.transpose(
                pooled_t[:, t * samples : (t + 1) * samples]
            ).astype(BF)
        if index < n_grp - 1:
            push(
                pooled_out.at[chunk], stacked.at[:, table_lanes(grp)], p_sem.at[0], p_sem.at[1], {"grp": chunk}
            ).start()
    stacked[:, table_lanes(grp)] = pooled_out[grp]

    for step in range(len(down_steps)):
        serve_down(step + 1)
        if step == len(down_steps) - 2:
            each(0, chosen.shape[1] // LANES, fill)
        serve_up(step)
        lay_up(step)
        lay_down(step)
    up_drain()
    down_drain()

    def down_round(i):
        at = pl.ds(pl.multiple_of(i * LANES, LANES), LANES)
        for j in range(rank // LANES):
            down[at, j * LANES : (j + 1) * LANES] = down32[j, at, :].astype(BF)

    each(0, columns // LANES, down_round)
    rows_moved.wait_send()
    bytes_of(stacked.at[:, width : width + 2 * width * (n_grp - 1)], p_sem).wait()

    def bias_at(at):
        return small[:, at]

    def head_at(start, size):
        if isinstance(start, int):
            return small[:, columns + start : columns + start + size]
        return small[:, pl.ds(pl.multiple_of(columns + start, LANES), size)]

    low_rank = jnp.dot(stacked[...], down[...], preferred_element_type=F32).astype(BF)
    partial = jnp.zeros((samples, LANES), F32)
    for k in range(columns // LANES):
        at = slice(k * LANES, (k + 1) * LANES)
        wide = stacked[:, at].astype(F32)
        part = jnp.dot(low_rank, up[:, at], preferred_element_type=F32) + bias_at(at)
        gain[:, at] = part
        partial = partial + (wide * part + wide) * head_at(k * LANES, LANES)
    logits = jnp.sum(jnp.transpose(partial), axis=0, keepdims=True)
    logits_ref[...] = logits
    residual = jax.nn.sigmoid(logits) - small[:, 2 * columns :]
    residual = jnp.transpose(jnp.broadcast_to(residual, (LANES, samples)))
    low_grad = jnp.zeros((samples, rank), F32)
    for k in range(columns // LANES):
        at = slice(k * LANES, (k + 1) * LANES)
        d_crossed = residual * head_at(k * LANES, LANES)
        d_gain = (d_crossed * stacked[:, at].astype(F32)).astype(BF)
        low_grad = low_grad + lax.dot_general(
            d_gain, up[:, at], (((1,), (1,)), ((), ())), preferred_element_type=F32
        )
    d_low[...] = low_grad.astype(BF)

    def place_of(index):
        return order.index((n_grp - order[index]) % n_grp)

    def lying(index):
        return d_in.at[pl.ds(index * 2 * samples, 2 * samples)]

    for index in range(n_grp):
        other = chunk_of(index)
        at = table_lanes(other)
        back = lax.dot_general(
            d_low[...], down[at, :], (((1,), (1,)), ((), ())), preferred_element_type=F32
        )
        d_crossed = jnp.concatenate([residual, residual], axis=1) * head_at(width + 2 * width * other, 2 * width)
        d_both = (d_crossed * (gain[:, at] + 1.0) + back).astype(BF)
        if index < n_grp - 1:
            place = place_of(index)
            d_out[index, :samples] = d_both[:, :width]
            d_out[index, samples:] = d_both[:, width:]
            push(d_out.at[index], lying(place), g_send, g_recv.at[place], {"grp": other}).start()
        else:
            d_in[index * 2 * samples : index * 2 * samples + samples] = d_both[:, :width]
            d_in[index * 2 * samples + samples :] = d_both[:, width:]

    parts = GRADIENT_PARTS[n_grp]

    def grad_rows(start, stop, part, first, last, out):
        def tile_step(at):
            lanes = lanes_of(*part)
            total = jnp.dot(counts[at, lanes], d_in[lanes, :], preferred_element_type=F32)
            if not first:
                total = slot_grad[at, :] + total
            if last:
                out(at, total.astype(BF))
            else:
                slot_grad[at, :] = total

        for begin in range(start, stop, GRADIENT_TILE):
            tile_step(slice(begin, min(stop, begin + GRADIENT_TILE)))

    def hot_done(at, value):
        hot_grad[at, :] = value

    def cold_done(at, value):
        rows = slice((at.start - hot_count) // cap, (at.stop - hot_count) // cap)
        cold_grad[rows] = value.reshape(rows.stop - rows.start, cap, width)

    def wait_for(part):
        for index in range(*part):
            if index < n_grp - 1:
                push(d_out.at[index], lying(index), g_send, g_recv.at[index], {"grp": grp}).wait_recv()

    for number, part in enumerate(parts[:-1]):
        wait_for(part)
        grad_rows(0, slot_total, part, number == 0, False, None)
    wait_for(parts[-1])
    only = len(parts) == 1
    grad_rows(0, hot_count, parts[-1], only, True, hot_done)

    per_half = hot_count // nc
    per_quarter = per_half // nx
    per_chip = per_quarter // ny

    def half_at(c):
        return pl.ds(pl.multiple_of(c * per_half, per_half), per_half)

    def quarter_at(x_):
        return pl.ds(pl.multiple_of(x_ * per_quarter, per_quarter), per_quarter)

    def chip_at(y_):
        return pl.ds(pl.multiple_of(y_ * per_chip, per_chip), per_chip)

    def total_quarter(x_):
        return pl.ds(pl.multiple_of(core * per_half + x_ * per_quarter, per_quarter), per_quarter)

    pair = push(hot_grad.at[half_at(1 - core)], pair_in, pair_sem.at[0], pair_sem.at[1], sibling)
    pair.start()
    grad_rows(hot_count, slot_total, parts[-1], only, True, cold_done)

    def cold_copy(other):
        return push(cold_grad.at[other], cold_in.at[me], c_sem.at[0], c_sem.at[1], {"wide": other})

    pair.wait()
    half[...] = (hot_grad[half_at(core), :].astype(F32) + pair_in[...].astype(F32)).astype(BF)
    for step in range(1, nx):
        to = lax.rem(x + step, nx)
        push(half.at[quarter_at(to)], x_in.at[x], xrs_sem.at[0], xrs_sem.at[1], at_wide(to, y)).start()
    x_in[x] = half[quarter_at(x), :]
    bytes_of(x_in.at[pl.ds(0, nx - 1)], xrs_sem).wait()
    quarter[...] = sum(x_in[x_].astype(F32) for x_ in range(nx)).astype(BF)
    for step in range(1, ny):
        to = lax.rem(y + step, ny)
        push(quarter.at[chip_at(to)], y_in.at[y], yrs_sem.at[0], yrs_sem.at[1], at_wide(x, to)).start()
    each(1, n_wide, lambda step: cold_copy(lax.rem(me + step, n_wide)).start())
    cold_in[me] = cold_grad[me]
    y_in[y] = quarter[chip_at(y), :]
    bytes_of(y_in.at[pl.ds(0, ny - 1)], yrs_sem).wait()
    mine = pl.ds(pl.multiple_of(core * per_half + x * per_quarter + y * per_chip, per_chip), per_chip)
    total_ref[mine, :] = sum(y_in[y_].astype(F32) for y_ in range(ny)).astype(BF)
    for step in range(1, ny):
        push(
            total_ref.at[mine], total_ref.at[mine], yag_sem.at[0], yag_sem.at[1], at_wide(x, lax.rem(y + step, ny))
        ).start()
    bytes_of(y_in.at[pl.ds(0, ny - 1)], yag_sem).wait()

    def to_sibling(x_):
        held = total_ref.at[total_quarter(x_)]
        return push(held, held, sib_send, sib_recv.at[x_], sibling)

    own = total_ref.at[total_quarter(x)]
    for step in range(1, nx):
        push(own, own, xag_send, xag_recv.at[x], at_wide(lax.rem(x + step, nx), y)).start()
    to_sibling(x).start()

    bytes_of(cold_in.at[pl.ds(0, n_wide - 1)], c_sem).wait()
    cold_sum_ref[...] = jnp.dot(
        chosen[...], cold_in[...].reshape(chosen.shape[1], LANES), preferred_element_type=F32
    )

    for step in range(1, nx):
        x_ = lax.rem(x + step, nx)
        held = total_ref.at[total_quarter(x_)]
        push(held, held, xag_send, xag_recv.at[x_], sibling).wait_recv()
        to_sibling(x_).start()
    for step in range(nx):
        to_sibling(lax.rem(x + step, nx)).wait_recv()
    sent = half.at[pl.ds(0, per_quarter * (nx - 1))]
    push(sent, sent, xag_send, xag_recv.at[0], sibling).wait_send()
    push(half, half, sib_send, sib_recv.at[0], sibling).wait_send()
    sent = d_out.at[pl.ds(0, n_grp - 1)]
    push(sent, sent, g_send, g_recv.at[0], sibling).wait_send()


def adagrad_kernel(
    logits_in, hot_grad, cold_grad, hot_ref, hot_accum, cold_ref, cold_accum,
    logits_ref, new_hot, new_hot_accum, new_cold, new_cold_accum,
):
    logits_ref[...] = logits_in[...]
    diagonal = (
        lax.broadcasted_iota(jnp.int32, (LANES, LANES), 0) == lax.broadcasted_iota(jnp.int32, (LANES, LANES), 1)
    )
    for grad_ref, rows_ref, accum_ref, new_rows, new_accum in (
        (hot_grad, hot_ref, hot_accum, new_hot, new_hot_accum),
        (cold_grad, cold_ref, cold_accum, new_cold, new_cold_accum),
    ):
        for start in range(0, rows_ref.shape[0], LANES):
            at = slice(start, start + LANES)
            gradient = grad_ref[at, :].astype(F32)
            old = jnp.sum(jnp.where(diagonal, accum_ref[:, at], 0.0), axis=1, keepdims=True)
            column = old + jnp.sum(gradient * gradient, axis=1, keepdims=True) / LANES
            new_accum[:, at] = jnp.sum(jnp.where(diagonal, column, 0.0), axis=0, keepdims=True)
            new_rows[at, :] = rows_ref[at, :] - gradient * (LEARN / (jnp.sqrt(column) + EPSILON))


VMEM = pl.BlockSpec(memory_space=pltpu.VMEM)
ANY = pl.BlockSpec(memory_space=pl.ANY)
DMA = pltpu.SemaphoreType.DMA


def on_device(
    n_wide, n_grp,
    dense_features, bag_slots, cold_offset, hot_rows, hot_accum, cold_rows, cold_accum,
    cross_down, cross_up, cross_bias, out_weight, labels,
):
    nx, ny, nc = wide_shape(n_wide)
    samples, width = dense_features.shape
    hot_count = hot_rows.shape[1]
    owned = cold_rows.shape[1]
    cap = cold_offset.shape[3]
    requests = n_wide * cap
    slot_total = hot_count + requests
    down_rows, rank = cross_down.shape
    up_rows, columns = cross_up.shape
    shard_rows = round_up(max(down_rows * rank, up_rows * columns) // LANES, 16)
    slots = jnp.transpose(bag_slots, (0, 2, 1))
    per_half = hot_count // nc
    per_quarter = per_half // nx

    def vm(*shape, dtype=BF):
        return pltpu.VMEM(shape, dtype)

    logits, hot_grad, cold_grad = pl.pallas_call(
        functools.partial(step_kernel, n_wide, n_grp),
        out_shape=(
            jax.ShapeDtypeStruct((1, samples), F32),
            jax.ShapeDtypeStruct((hot_count, width), BF),
            jax.ShapeDtypeStruct((owned, width), F32),
        ),
        in_specs=[VMEM, ANY, VMEM, VMEM, VMEM, ANY, VMEM, VMEM, VMEM, VMEM],
        out_specs=(VMEM,) * 3,
        scratch_shapes=[
            vm(owned, width, dtype=F32), vm(hot_count, width, dtype=F32), vm(1, 2 * columns + samples, dtype=F32),
            vm(LANES, LANES, dtype=F32), vm(n_wide, LANES, dtype=F32), vm(n_wide, LANES, dtype=F32),
            vm(requests // LANES, LANES, dtype=jnp.int32),
            vm(owned, width), vm(n_wide, cap, width), vm(n_wide, cap, width),
            vm(shard_rows, LANES, dtype=F32), vm(shard_rows, LANES), vm(shard_rows, LANES),
            vm(ny, nc, nx, shard_rows, LANES), vm(nx, nc, ny, shard_rows, LANES),
            vm(rank // LANES, columns, LANES, dtype=F32), vm(columns, rank), vm(rank, columns),
            vm(width, slot_total), vm(slot_total, n_grp * 2 * samples),
            vm(n_grp, width, 2 * samples, dtype=F32), vm(n_grp, samples, 2 * width),
            vm(samples, columns), vm(samples, columns, dtype=F32), vm(samples, rank),
            vm(n_grp, 2 * samples, width), vm(n_grp * 2 * samples, width), vm(slot_total, width, dtype=F32),
            vm(hot_count, width), vm(n_wide, cap, width), vm(n_wide, cap, width),
            vm(per_half, width), vm(per_half, width), vm(nx, per_quarter, width),
            vm(per_quarter, width), vm(ny, per_quarter // ny, width),
            vm(owned, requests),
        ]
        + [DMA((2,))] * 11
        + [DMA((3,)), DMA((ny,)), DMA((ny,)), DMA((ny,)), DMA((3,)), DMA((nx,)), DMA((nx,)), DMA((nx,))]
        + [DMA, DMA((n_grp,)), DMA, DMA((nx,)), DMA, DMA((nx,))],
        compiler_params=pltpu.CompilerParams(
            collective_id=0, has_side_effects=True, vmem_limit_bytes=60 * 1024 * 1024
        ),
        name="train_step",
    )(
        jnp.transpose(cold_offset[0, 0]), cold_rows[0], cross_down, cross_up, slots, hot_rows[0], dense_features,
        cross_bias, out_weight, labels,
    )

    steps = 2 if hot_count % (2 * LANES) == 0 and owned % (2 * LANES) == 0 else 1
    hot_block, cold_block = hot_count // steps, owned // steps

    def rows_spec(size):
        return pl.BlockSpec((size, width), lambda i: (i, 0))

    def accum_spec(size):
        return pl.BlockSpec((1, size), lambda i: (0, i))

    whole = pl.BlockSpec((1, samples), lambda i: (0, 0))
    logits, new_hot, new_hot_accum, new_cold, new_cold_accum = pl.pallas_call(
        adagrad_kernel,
        grid=(steps,),
        out_shape=(
            jax.ShapeDtypeStruct((1, samples), F32),
            jax.ShapeDtypeStruct((hot_count, width), F32),
            jax.ShapeDtypeStruct((1, hot_count), F32),
            jax.ShapeDtypeStruct((owned, width), F32),
            jax.ShapeDtypeStruct((1, owned), F32),
        ),
        in_specs=[
            whole, rows_spec(hot_block), rows_spec(cold_block),
            rows_spec(hot_block), accum_spec(hot_block), rows_spec(cold_block), accum_spec(cold_block),
        ],
        out_specs=(whole, rows_spec(hot_block), accum_spec(hot_block), rows_spec(cold_block), accum_spec(cold_block)),
        name="adagrad",
    )(logits, hot_grad, cold_grad, hot_rows[0], hot_accum, cold_rows[0], cold_accum)
    return (logits.reshape(samples), new_hot[None], new_hot_accum, new_cold[None], new_cold_accum)


def solution(mesh):
    return jax.shard_map(
        functools.partial(on_device, mesh.shape["wide"], mesh.shape["grp"]),
        mesh=mesh,
        in_specs=(
            P(("wide", "grp"), None),
            P("grp", "wide", None),
            P("grp", "wide", None, None),
            P("grp", None, None),
            P("grp", None),
            P("grp", "wide", None),
            P("grp", "wide"),
            P("wide", None),
            P("wide", None),
            P(),
            P(),
            P(("wide", "grp")),
        ),
        out_specs=(
            P(("wide", "grp")),
            P("grp", None, None),
            P("grp", None),
            P("grp", "wide", None),
            P("grp", "wide"),
        ),
        check_vma=False,
    )
```

time: 118 us -> 103 us (0.87)
  Pallas kernels: 115 us -> 102 us
  local copies, waits for them, and re-layouts: 1.42 us -> 0 us
    pallas_call x1, Pallas kernels: 109 us -> 98.5 us  [on_device(): pl.pallas_call(functools.partial(step_kernel, n_wide, n_grp), out_shape=(...]
    pallas_call x1, Pallas kernels: 6.52 us -> 3.29 us  [on_device(): pl.pallas_call(adagrad_kernel, grid=(steps,), out_shape=(jax.ShapeDtypeSt...]
where the time goes in v3:
time: 103 us; the launch traced here: 102 us
  Pallas kernels  102 us (99%)
    pallas_call x1, Pallas kernels, on_device(): pl.pallas_call(functools.partial(step_kernel, n_wide, n_grp), out_shape=(...  98.5 us
    pallas_call x1, Pallas kernels, on_device(): pl.pallas_call(adagrad_kernel, grid=(steps,), out_shape=(jax.ShapeDtypeSt...  3.29 us

profile of v3, /device:TPU:1, one launch (start us, length us, event | category | flops | bytes accessed | tf_op | source)
XLA Modules:
  0.0 102.4 jit_solution(3249177098402581451)
XLA Ops:
  0.6 98.5 %train_step.1 = (f32[1,128]{1,0:T(1,128)}, bf16[2048,128]{1,0:T(8,128)(2,1)}, f32[1024,128]{1,0:T(8,128)}) custom-call(s32[16,64]{1,0:T(8,128)} %bitcast.14, f32[1024,128]{1,0:T(8,128)} %bitcast.11, bf16[34,512]{1,0:T(8,128)(2,1)} %down_ref.1, bf16[8,2176]{1,0:T(8,128)(2,1)} %up_ref.1, s32[2,8,1024]{2,1,0:T(8,128)} %bitcast.13, f32[2048,128]{1,0:T(8,128)} %bitcast.9, ...), custom_call_target="tpu_custom_call" | custom-call | tf_op jit(solution)/shard_map/train_step/pallas_call | solution.py:576
  99.1 3.3 %adagrad.1 = (f32[1,128]{1,0:T(1,128)}, f32[2048,128]{1,0:T(8,128)}, f32[1,2048]{1,0:T(1,128)}, f32[1024,128]{1,0:T(8,128)}, f32[1,1024]{1,0:T(1,128)}) custom-call(f32[1,128]{1,0:T(1,128)} %get-tuple-element.13.logits_in, bf16[2048,128]{1,0:T(8,128)(2,1)} %get-tuple-element.14.hot_grad, f32[1024,128]{1,0:T(8,128)} %get-tuple-element.15.cold_grad, ...), custom_call_target="tpu_custom_call" | custom-call | tf_op jit(solution)/shard_map/adagrad/pallas_call | solution.py:624

commit v4 on v3

--- a/solution.py
+++ b/solution.py
@@ -17,7 +17,7 @@
 
 
 def wide_shape(n_wide):
-    return {64: (4, 8, 2), 8: (2, 2, 2)}[n_wide]
+    return {64: (4, 8, 2), 16: (2, 4, 2), 8: (2, 2, 2)}[n_wide]
 
 
 def round_up(value, unit):
@@ -50,13 +50,13 @@
 def step_kernel(
     n_wide, n_grp,
     offset_ref, cold_hbm, down_ref, up_ref, slots_ref, hot_hbm, dense_ref, bias_ref, head_ref, labels_ref,
-    logits_ref, total_ref, cold_sum_ref,
+    logits_ref, total_ref, cold_sum_hbm,
     cold_ref, hot_ref, small, square, ask, asked, asked_lane, cold_bf, picked, fetched,
     shard32, shard_down, shard_up, all_down, all_up, down32, down, up,
     buffer_t, counts, pooled_hot, pooled_out, stacked, gain, d_low, d_out, d_in, slot_grad,
-    hot_grad, cold_grad, cold_in, pair_in, half, x_in, quarter, y_in, chosen,
-    load_sem, ask_sem, row_sem, d1_sem, u1_sem, p_sem, c_sem, pair_sem, xrs_sem, yrs_sem, yag_sem,
-    d_send, d_fwd, d_bwd, d_side, u_send, u_fwd, u_bwd, u_side, g_send, g_recv, xag_send, xag_recv, sib_send, sib_recv,
+    hot_grad, cold_grad, cold_in, pair_in, half, piece_in, far_in, cold_sum, chosen,
+    load_sem, ask_sem, row_sem, d1_sem, u1_sem, p_sem, c_sem, pair_sem, prs_sem, far_sem,
+    d_send, d_fwd, d_bwd, d_side, u_send, u_fwd, u_bwd, u_side, g_send, g_recv, back_send, back_recv, sib_send, sib_recv,
 ):
     nx, ny, nc = wide_shape(n_wide)
     chips = nx * ny
@@ -321,6 +321,8 @@
     asks.wait_send()
     rows_moved = bytes_of(picked.at[pl.ds(0, n_wide - 1)], row_sem)
     rows_moved.wait_recv()
+    serve_down(1)
+    serve_up(0)
     for k in range((slot_total - hot_count) // LANES):
         part = jnp.concatenate([fetched[k * per_batch + i] for i in range(per_batch)], axis=0).astype(F32)
         at = hot_count + k * LANES
@@ -344,11 +346,13 @@
             ).start()
     stacked[:, table_lanes(grp)] = pooled_out[grp]
 
+    serve_down(2)
     for step in range(len(down_steps)):
-        serve_down(step + 1)
+        if step == 1:
+            serve_down(3)
         if step == len(down_steps) - 2:
             each(0, chosen.shape[1] // LANES, fill)
-        serve_up(step)
+        serve_up(step + 1)
         lay_up(step)
         lay_down(step)
     up_drain()
@@ -452,20 +456,23 @@
     grad_rows(0, hot_count, parts[-1], only, True, hot_done)
 
     per_half = hot_count // nc
-    per_quarter = per_half // nx
-    per_chip = per_quarter // ny
+    members = nx * 2
+    per_piece = per_half // members
+    pairs = ny // 2
+    pair_row, low_row = y // 2, lax.rem(y, 2)
+    mine = x * 2 + low_row
 
     def half_at(c):
         return pl.ds(pl.multiple_of(c * per_half, per_half), per_half)
 
-    def quarter_at(x_):
-        return pl.ds(pl.multiple_of(x_ * per_quarter, per_quarter), per_quarter)
-
-    def chip_at(y_):
-        return pl.ds(pl.multiple_of(y_ * per_chip, per_chip), per_chip)
-
-    def total_quarter(x_):
-        return pl.ds(pl.multiple_of(core * per_half + x_ * per_quarter, per_quarter), per_quarter)
+    def piece_at(k):
+        return pl.ds(pl.multiple_of(k * per_piece, per_piece), per_piece)
+
+    def total_at(k):
+        return total_ref.at[pl.ds(pl.multiple_of(core * per_half + k * per_piece, per_piece), per_piece)]
+
+    def member(k):
+        return at_wide(k // 2, pair_row * 2 + lax.rem(k, 2))
 
     pair = push(hot_grad.at[half_at(1 - core)], pair_in, pair_sem.at[0], pair_sem.at[1], sibling)
     pair.start()
@@ -476,53 +483,48 @@
 
     pair.wait()
     half[...] = (hot_grad[half_at(core), :].astype(F32) + pair_in[...].astype(F32)).astype(BF)
-    for step in range(1, nx):
-        to = lax.rem(x + step, nx)
-        push(half.at[quarter_at(to)], x_in.at[x], xrs_sem.at[0], xrs_sem.at[1], at_wide(to, y)).start()
-    x_in[x] = half[quarter_at(x), :]
-    bytes_of(x_in.at[pl.ds(0, nx - 1)], xrs_sem).wait()
-    quarter[...] = sum(x_in[x_].astype(F32) for x_ in range(nx)).astype(BF)
-    for step in range(1, ny):
-        to = lax.rem(y + step, ny)
-        push(quarter.at[chip_at(to)], y_in.at[y], yrs_sem.at[0], yrs_sem.at[1], at_wide(x, to)).start()
+    for step in range(1, members):
+        to = lax.rem(mine + step, members)
+        push(half.at[piece_at(to)], piece_in.at[mine], prs_sem.at[0], prs_sem.at[1], member(to)).start()
+    piece_in[mine] = half[piece_at(mine), :]
+    bytes_of(piece_in.at[pl.ds(0, members - 1)], prs_sem).wait()
+    far_in[pair_row] = sum(piece_in[k].astype(F32) for k in range(members)).astype(BF)
+    held = far_in.at[pair_row]
+    for step in range(1, pairs):
+        to = at_wide(x, lax.rem(pair_row + step, pairs) * 2 + low_row)
+        push(held, held, far_sem.at[0], far_sem.at[1], to).start()
     each(1, n_wide, lambda step: cold_copy(lax.rem(me + step, n_wide)).start())
     cold_in[me] = cold_grad[me]
-    y_in[y] = quarter[chip_at(y), :]
-    bytes_of(y_in.at[pl.ds(0, ny - 1)], yrs_sem).wait()
-    mine = pl.ds(pl.multiple_of(core * per_half + x * per_quarter + y * per_chip, per_chip), per_chip)
-    total_ref[mine, :] = sum(y_in[y_].astype(F32) for y_ in range(ny)).astype(BF)
-    for step in range(1, ny):
-        push(
-            total_ref.at[mine], total_ref.at[mine], yag_sem.at[0], yag_sem.at[1], at_wide(x, lax.rem(y + step, ny))
-        ).start()
-    bytes_of(y_in.at[pl.ds(0, ny - 1)], yag_sem).wait()
-
-    def to_sibling(x_):
-        held = total_ref.at[total_quarter(x_)]
-        return push(held, held, sib_send, sib_recv.at[x_], sibling)
-
-    own = total_ref.at[total_quarter(x)]
-    for step in range(1, nx):
-        push(own, own, xag_send, xag_recv.at[x], at_wide(lax.rem(x + step, nx), y)).start()
-    to_sibling(x).start()
+    if pairs > 1:
+        bytes_of(far_in.at[pl.ds(0, pairs - 1)], far_sem).wait()
+    total_at(mine)[...] = sum(far_in[k].astype(F32) for k in range(pairs)).astype(BF)
+
+    def to_sibling(k):
+        return push(total_at(k), total_at(k), sib_send, sib_recv.at[k], sibling)
+
+    for step in range(1, members):
+        push(total_at(mine), total_at(mine), back_send, back_recv.at[mine], member(lax.rem(mine + step, members))).start()
+    to_sibling(mine).start()
 
     bytes_of(cold_in.at[pl.ds(0, n_wide - 1)], c_sem).wait()
-    cold_sum_ref[...] = jnp.dot(
+    cold_sum[...] = jnp.dot(
         chosen[...], cold_in[...].reshape(chosen.shape[1], LANES), preferred_element_type=F32
     )
-
-    for step in range(1, nx):
-        x_ = lax.rem(x + step, nx)
-        held = total_ref.at[total_quarter(x_)]
-        push(held, held, xag_send, xag_recv.at[x_], sibling).wait_recv()
-        to_sibling(x_).start()
-    for step in range(nx):
-        to_sibling(lax.rem(x + step, nx)).wait_recv()
-    sent = half.at[pl.ds(0, per_quarter * (nx - 1))]
-    push(sent, sent, xag_send, xag_recv.at[0], sibling).wait_send()
+    cold_out = pltpu.make_async_copy(cold_sum, cold_sum_hbm, load_sem.at[0])
+    cold_out.start()
+
+    for step in range(1, members):
+        k = lax.rem(mine + step, members)
+        push(total_at(k), total_at(k), back_send, back_recv.at[k], sibling).wait_recv()
+        to_sibling(k).start()
+    for step in range(members):
+        to_sibling(lax.rem(mine + step, members)).wait_recv()
+    sent = half.at[pl.ds(0, per_piece * (members - 1))]
+    push(sent, sent, back_send, back_recv.at[0], sibling).wait_send()
     push(half, half, sib_send, sib_recv.at[0], sibling).wait_send()
     sent = d_out.at[pl.ds(0, n_grp - 1)]
     push(sent, sent, g_send, g_recv.at[0], sibling).wait_send()
+    cold_out.wait()
 
 
 def adagrad_kernel(
@@ -568,7 +570,7 @@
     shard_rows = round_up(max(down_rows * rank, up_rows * columns) // LANES, 16)
     slots = jnp.transpose(bag_slots, (0, 2, 1))
     per_half = hot_count // nc
-    per_quarter = per_half // nx
+    members = nx * 2
 
     def vm(*shape, dtype=BF):
         return pltpu.VMEM(shape, dtype)
@@ -581,7 +583,7 @@
             jax.ShapeDtypeStruct((owned, width), F32),
         ),
         in_specs=[VMEM, ANY, VMEM, VMEM, VMEM, ANY, VMEM, VMEM, VMEM, VMEM],
-        out_specs=(VMEM,) * 3,
+        out_specs=(VMEM, VMEM, ANY),
         scratch_shapes=[
             vm(owned, width, dtype=F32), vm(hot_count, width, dtype=F32), vm(1, 2 * columns + samples, dtype=F32),
             vm(LANES, LANES, dtype=F32), vm(n_wide, LANES, dtype=F32), vm(n_wide, LANES, dtype=F32),
@@ -595,13 +597,12 @@
             vm(samples, columns), vm(samples, columns, dtype=F32), vm(samples, rank),
             vm(n_grp, 2 * samples, width), vm(n_grp * 2 * samples, width), vm(slot_total, width, dtype=F32),
             vm(hot_count, width), vm(n_wide, cap, width), vm(n_wide, cap, width),
-            vm(per_half, width), vm(per_half, width), vm(nx, per_quarter, width),
-            vm(per_quarter, width), vm(ny, per_quarter // ny, width),
-            vm(owned, requests),
+            vm(per_half, width), vm(per_half, width), vm(members, per_half // members, width),
+            vm(ny // 2, per_half // members, width), vm(owned, width, dtype=F32), vm(owned, requests),
         ]
-        + [DMA((2,))] * 11
+        + [DMA((2,))] * 10
         + [DMA((3,)), DMA((ny,)), DMA((ny,)), DMA((ny,)), DMA((3,)), DMA((nx,)), DMA((nx,)), DMA((nx,))]
-        + [DMA, DMA((n_grp,)), DMA, DMA((nx,)), DMA, DMA((nx,))],
+        + [DMA, DMA((n_grp,)), DMA, DMA((members,)), DMA, DMA((members,))],
         compiler_params=pltpu.CompilerParams(
             collective_id=0, has_side_effects=True, vmem_limit_bytes=60 * 1024 * 1024
         ),

time: 103 us -> 97.3 us (0.945)
  Pallas kernels: 102 us -> 96.5 us
    pallas_call x1, Pallas kernels: 98.5 us -> 93.2 us  [on_device(): pl.pallas_call(functools.partial(step_kernel, n_wide, n_grp), out_shape=(...]
where the time goes in v4:
time: 97.3 us; the launch traced here: 97.1 us
  Pallas kernels  96.5 us (99%)
    pallas_call x1, Pallas kernels, on_device(): pl.pallas_call(functools.partial(step_kernel, n_wide, n_grp), out_shape=(...  93.2 us
    pallas_call x1, Pallas kernels, on_device(): pl.pallas_call(adagrad_kernel, grid=(steps,), out_shape=(jax.ShapeDtypeSt...  3.29 us

profile of v4, /device:TPU:1, one launch (start us, length us, event | category | flops | bytes accessed | tf_op | source)
XLA Modules:
  0.0 97.1 jit_solution(14334038348876217136)
XLA Ops:
  0.6 93.2 %train_step.1 = (f32[1,128]{1,0:T(1,128)}, bf16[2048,128]{1,0:T(8,128)(2,1)}, f32[1024,128]{1,0:T(8,128)}) custom-call(s32[16,64]{1,0:T(8,128)} %bitcast.14, f32[1024,128]{1,0:T(8,128)} %bitcast.11, bf16[34,512]{1,0:T(8,128)(2,1)} %down_ref.1, bf16[8,2176]{1,0:T(8,128)(2,1)} %up_ref.1, s32[2,8,1024]{2,1,0:T(8,128)} %bitcast.13, f32[2048,128]{1,0:T(8,128)} %bitcast.9, ...), custom_call_target="tpu_custom_call" | custom-call | tf_op jit(solution)/shard_map/train_step/pallas_call | solution.py:578
  93.8 3.3 %adagrad.1 = (f32[1,128]{1,0:T(1,128)}, f32[2048,128]{1,0:T(8,128)}, f32[1,2048]{1,0:T(1,128)}, f32[1024,128]{1,0:T(8,128)}, f32[1,1024]{1,0:T(1,128)}) custom-call(f32[1,128]{1,0:T(1,128)} %get-tuple-element.13.logits_in, bf16[2048,128]{1,0:T(8,128)(2,1)} %get-tuple-element.14.hot_grad, f32[1024,128]{1,0:T(8,128)} %get-tuple-element.15.cold_grad, ...), custom_call_target="tpu_custom_call" | custom-call | tf_op jit(solution)/shard_map/adagrad/pallas_call | solution.py:625
